TPU v7x, 256 devices: a whole 4x4x8 slice. The times are simulated.
256 devices in a mesh: seq: 64 (over y, z_hi, x), head: 4 (over z_lo, core).
Axes of the slice: x: 4, y: 4, z: 8 (z_hi: 4, z_lo: 2; z = z_hi * 2 + z_lo), core: 2. Of those that a mesh axis runs over, the one named last changes fastest.
Arguments:
- tokens: bfloat16 [16384, 1536], P('seq'), may hold values from -200 to 200
- query_weight: bfloat16 [1536, 1536], P(None, 'head'), may hold values from -0.15625 to 0.15625
- key_weight: bfloat16 [1536, 1536], P(None, 'head'), may hold values from -0.15625 to 0.15625
- value_weight: bfloat16 [1536, 1536], P(None, 'head'), may hold values from -0.15625 to 0.15625
- offsets: int32 [4, 24], P(None, 'head'), may hold values from 0 to 7
- out_weight: bfloat16 [1536, 1536], P('head'), may hold values from -0.15625 to 0.15625
Outputs:
- layer_out: bfloat16 [16384, 1536], P(('seq', 'head'))
All inputs are finite; a program needn't handle non-finite values.
Results may differ from a plain program's by a relative error of at most 0.0095.
The roundings to bfloat16 on the way count: a program that leaves them out, or rounds other values in their place, can miss the bound.
Values may be sent and summed in bfloat16 or wider, within the bound.
A program may use at most 64 MiB of HBM per device.

v0:
```python
import jax
import jax.numpy as jnp
from jax import lax
from jax.sharding import PartitionSpec as P

HDIM = 64
LEVELS = 4


score_scale = 0.125
absent_value = -1e30


def partner_2(x, axis, distance):
    return lax.ppermute(x, axis, [(i, i ^ 1 << distance) for i in range(lax.axis_size(axis))])


def select(values, stride, offset):
    shaped = values.reshape(values.shape[0] // stride, stride, values.shape[1], values.shape[2])
    picker = (jnp.arange(stride, dtype=jnp.int32)[:, None] == offset[None, :]).astype(values.dtype)
    return jnp.sum(shaped * picker[None, :, :, None], axis=1)


def attend(triple):
    query_set, key_set, value_set = triple
    scores = jnp.dot(query_set, key_set.T, preferred_element_type=jnp.float32) * score_scale
    row_max = jnp.max(scores, axis=1)
    probs = jnp.exp(scores - row_max[:, None])
    total = jnp.sum(probs, axis=1)
    mixed = (
        jnp.dot(probs.astype(jnp.bfloat16), value_set, preferred_element_type=jnp.float32)
        / total[:, None]
    )
    return (mixed, row_max + jnp.log(total))


def double_up(gathered, partner, bit_no, my_index):
    upper = my_index // 2**bit_no % 2
    return jnp.where(
        upper == 1, jnp.concatenate([partner, gathered], 0), jnp.concatenate([gathered, partner], 0)
    )


def swap_level(gathered, bit_no):
    return partner_2(gathered, "seq", bit_no)


def local(tokens, query_weight, key_weight, value_weight, offsets, out_weight):
    tok_rows = tokens.shape[0]
    local_width = query_weight.shape[1]
    local_heads = local_width // HDIM

    def project(weight):
        return (
            jnp.dot(tokens, weight, preferred_element_type=jnp.float32)
            .astype(jnp.bfloat16)
            .reshape(tok_rows, local_heads, HDIM)
        )

    queries = project(query_weight)
    key_rows = project(key_weight)
    value_rows = project(value_weight)
    seq_count = lax.axis_size("seq")
    log_count = seq_count.bit_length() - 1
    my_index = lax.axis_index("seq")
    strides = [2**level_no for level_no in range(LEVELS)]
    level_bits = [log_count - 3 + level_no for level_no in range(LEVELS)]
    level_offsets = [offsets[level_no] % strides[level_no] for level_no in range(LEVELS)]
    kept_queries = []
    pending = []
    for level_no in range(LEVELS):
        stride = strides[level_no]
        kept_queries.append(select(queries, stride, level_offsets[level_no]))
        kept_keys = select(key_rows, stride, level_offsets[level_no]).reshape(
            tok_rows // stride, local_width
        )
        kept_values = select(value_rows, stride, level_offsets[level_no]).reshape(
            tok_rows // stride, local_width
        )
        pending.append(jnp.concatenate([kept_keys, kept_values], 1))
    for level_no in range(LEVELS):
        for bit_no in range(level_bits[level_no]):
            partner = swap_level(pending[level_no], bit_no)
            pending[level_no] = double_up(pending[level_no], partner, bit_no, my_index)
    mixed_all = []
    log_all = []
    for level_no in range(LEVELS):
        stride = strides[level_no]
        gathered = pending[level_no]
        span_rows = gathered.shape[0]
        key_heads = (
            gathered[:, :local_width].reshape(span_rows, local_heads, HDIM).transpose(1, 0, 2)
        )
        value_heads = (
            gathered[:, local_width:].reshape(span_rows, local_heads, HDIM).transpose(1, 0, 2)
        )
        query_heads = kept_queries[level_no].transpose(1, 0, 2)
        mixed, log_total = lax.map(attend, (query_heads, key_heads, value_heads))
        mixed = mixed.transpose(1, 0, 2)
        log_total = log_total.transpose(1, 0)
        picker = jnp.arange(stride, dtype=jnp.int32)[:, None] == level_offsets[level_no][None, :]
        full_mixed = mixed[:, None, :, :] * picker[None, :, :, None].astype(jnp.float32)
        full_log = jnp.where(picker[None, :, :], log_total[:, None, :], jnp.float32(absent_value))
        mixed_all.append(full_mixed.reshape(tok_rows, local_heads, HDIM))
        log_all.append(full_log.reshape(tok_rows, local_heads))
    stacked_log = jnp.stack(log_all)
    best = jnp.max(stacked_log, axis=0)
    weights = jnp.exp(stacked_log - best[None])
    weight_sum = jnp.sum(weights, axis=0)
    combined = sum(
        (weights[level_no][:, :, None] * mixed_all[level_no] for level_no in range(LEVELS))
    )
    attention = (
        (combined / weight_sum[:, :, None]).astype(jnp.bfloat16).reshape(tok_rows, local_width)
    )
    layer_out = lax.psum_scatter(
        jnp.dot(attention, out_weight, preferred_element_type=jnp.float32),
        "head",
        scatter_dimension=0,
        tiled=True,
    )
    return layer_out.astype(jnp.bfloat16)


def solution(mesh):
    return jax.shard_map(
        local,
        mesh=mesh,
        in_specs=(
            P("seq", None),
            P(None, "head"),
            P(None, "head"),
            P(None, "head"),
            P(None, "head"),
            P("head", None),
        ),
        out_specs=P(("seq", "head"), None),
        check_vma=False,
    )
```

profile of v0, /device:TPU:1, one launch (start us, length us, event | category | flops | bytes accessed | tf_op | source)
XLA Modules:
  0.0 497.7 jit_solution(10838936492549715647)
XLA Ops:
  6.5 2.2 convolution_convert_fusion
  10.2 2.0 collective-permute-start
  12.8 2.1 convolution_convert_fusion.2
  33.5 2.5 collective-permute-start.1
  38.3 16.0 %collective-permute-done.7 = bf16[64,768]{1,0:T(8,128)(2,1)S(1)} collective-permute-done((bf16[64,768]{1,0:T(8,128)(2,1)S(1)}, bf16[64,768]{1,0:T(8,128)(2,1)S(1)}, u32[]{:S(2)}, u32[]{:S(2)}) %collective-permute-start.7) | collective-permute-done | bytes 98336 | tf_op jit(solution)/shard_map/ppermute | solution.py:15
  54.4 2.3 collective-permute-done.13
  56.7 3.4 collective-permute-start.14
  61.2 2.5 collective-permute-start.4
  64.0 2.3 maximum_select_fusion.4
  66.2 2.4 collective-permute-start.2
  68.8 48.5 %collective-permute-start.15 = (bf16[256,768]{1,0:T(8,128)(2,1)S(1)}, bf16[256,768]{1,0:T(8,128)(2,1)}, u32[]{:S(2)}, u32[]{:S(2)}) collective-permute-start(bf16[256,768]{1,0:T(8,128)(2,1)S(1)} %maximum_select_fusion.14), channel_id=1, source_target_pairs={{0,32},{4,36},{8,40},{12,44},{16,48},{20,52},{24,56},{28,60},{32,0... | collective-permute-start | bytes 1179656 | tf_op jit(solution)/shard_map/ppermute | solution.py:15
  120.1 40.3 %collective-permute-start.10 = (bf16[512,768]{1,0:T(8,128)(2,1)}, bf16[512,768]{1,0:T(8,128)(2,1)}, u32[]{:S(2)}, u32[]{:S(2)}) collective-permute-start(bf16[512,768]{1,0:T(8,128)(2,1)} %maximum_select_fusion.10), channel_id=1, source_target_pairs={{0,32},{4,36},{8,40},{12,44},{16,48},{20,52},{24,56},{28,60},{32,0... | collective-permute-start | bytes 2359304 | tf_op jit(solution)/shard_map/ppermute | solution.py:15
  160.4 2.2 maximum_select_fusion.11
  171.2 49.5 %collective-permute-done.5 = bf16[512,768]{0,1:T(8,128)(2,1)} collective-permute-done((bf16[512,768]{0,1:T(8,128)(2,1)}, bf16[512,768]{0,1:T(8,128)(2,1)}, u32[]{:S(2)}, u32[]{:S(2)}) %collective-permute-start.5) | collective-permute-done | bytes 786464 | tf_op jit(solution)/shard_map/ppermute | solution.py:15
  220.6 3.6 maximum_select_fusion.5
  224.2 90.4 %collective-permute-start.6 = (bf16[1024,768]{0,1:T(8,128)(2,1)}, bf16[1024,768]{0,1:T(8,128)(2,1)}, u32[]{:S(2)}, u32[]{:S(2)}) collective-permute-start(bf16[1024,768]{0,1:T(8,128)(2,1)} %maximum_select_fusion.5), channel_id=1, source_target_pairs={{0,32},{4,36},{8,40},{12,44},{16,48},{20,52},{24,56},{28,60},{32,0... | collective-permute-start | bytes 4718600 | tf_op jit(solution)/shard_map/ppermute | solution.py:15
  314.7 3.4 maximum_select_fusion.6
  319.4 3.4 maximum_select_fusion.7
  322.7 2.6 collective-permute-start.17
  325.4 2.5 maximum_select_fusion
  329.3 2.7 copy.132
  332.0 1.7 copy.133
  333.7 24.5 %while.48 = (s32[]{:T(128)}, f32[6,256,64]{1,2,0:T(8,128)}, f32[6,256]{1,0:T(8,128)S(1)}, bf16[6,256,64]{1,2,0:T(8,128)(2,1)S(1)}, bf16[6,2048,64]{1,2,0:T(8,128...) while((s32[]{:T(128)}, f32[6,256,64]{1,2,0:T(8,128)}, f32[6,256]{1,0:T(8,128)S(1)}, ...), condition=%wide.region_3.4_spmd, body=%wide.region_0.0_spmd.sunk | while | flops 137379584 | bytes 6926425 | solution.py:98
  335.7 2.1 fusion.122
  339.7 2.1 fusion.122
  343.8 2.1 fusion.122
  347.9 2.1 fusion.122
  352.0 2.1 fusion.122
  356.1 2.1 fusion.122
  358.8 4.2 maximum_select_fusion.1
  363.1 2.1 fusion.85
  365.2 18.2 %while.49 = (s32[]{:T(128)}, f32[6,128,64]{1,2,0:T(8,128)S(1)}, f32[6,128]{1,0:T(8,128)S(1)}, bf16[6,128,64]{2,1,0:T(8,128)(2,1)}, bf16[6,2048,64]{1,2,0:T(8,128...) while((s32[]{:T(128)}, f32[6,128,64]{1,2,0:T(8,128)S(1)}, f32[6,128]{1,0:T(8,128)S(1)}, ...), condition=%wide.region_10.11_spmd, body=%wide.region_7.0_spmd.sunk | while | flops 68689792 | bytes 3742809 | solution.py:98
  385.6 3.4 maximum_select_fusion.2
  390.5 2.6 copy.144
  393.2 1.7 copy.145
  394.8 17.1 %while.50 = (s32[]{:T(128)}, f32[6,64,64]{2,1,0:T(8,128)S(1)}, f32[6,64]{1,0:T(8,128)S(1)}, bf16[6,64,64]{2,1,0:T(8,128)(2,1)}, bf16[6,2048,64]{1,2,0:T(8,128)(2...) while((s32[]{:T(128)}, f32[6,64,64]{2,1,0:T(8,128)S(1)}, f32[6,64]{1,0:T(8,128)S(1)}, ...), condition=%wide.region_17.18_spmd, body=%wide.region_14.17_spmd.sunk | while | flops 34344896 | bytes 2151513 | solution.py:98
  414.2 3.2 maximum_select_fusion.3
  418.8 2.6 copy.150
  423.2 27.6 %while.51 = (s32[]{:T(128)}, f32[6,32,64]{2,1,0:T(8,128)}, f32[6,32]{1,0:T(8,128)}, bf16[6,32,64]{2,1,0:T(8,128)(2,1)}, bf16[6,2048,64]{1,2,0:T(8,128)(2,1)}, /*...) while((s32[]{:T(128)}, f32[6,32,64]{2,1,0:T(8,128)}, f32[6,32]{1,0:T(8,128)}, ...), condition=%wide.region_24.25_spmd, body=%wide.region_21.24_spmd.sunk | while | flops 17172448 | bytes 1338713 | solution.py:98
  426.0 1.8 fusion.137
  430.6 1.8 fusion.137
  435.2 1.8 fusion.137
  439.8 1.8 fusion.137
  444.3 1.8 fusion.137
  448.9 1.8 fusion.137
  454.6 1.7 fusion.89
  456.3 32.8 %reduce-scatter.2.cloned.1.call-done = f32[64,1536]{1,0:T(8,128)} async-done(((f32[256,1536]{1,0:T(8,128)}), f32[64,1536]{1,0:T(8,128)}) %reduce-scatter.2.cloned.1.call-update) | async-done | bytes 393232 | tf_op jit(solution)/shard_map/reduce_scatter | solution.py:116
  489.2 1.7 convert_element_type.139
  (274 shorter events, 115.0 us)
Async XLA Ops:
  6.5 448.0 %copy-start = (bf16[384,1536]{1,0:T(8,128)(2,1)S(1)}, bf16[384,1536]{1,0:T(8,128)(2,1)}, u32[]{:S(2)}) copy-start(bf16[384,1536]{1,0:T(8,128)(2,1)} %param.19) | copy-start | bytes 3538948
  6.5 2.2 copy-start.22
  6.5 2.3 copy-start.21
  6.5 482.6 %reduce-scatter.2.cloned.1.call-start = ((), (), s32[]{:S(2)}) async-start(), calls=%async_computation.1 | async-start | bytes 1966080 | tf_op jit(solution)/shard_map/reduce_scatter | solution.py:116
  10.2 22.0 %collective-permute-start = (bf16[256,768]{1,0:T(8,128)(2,1)}, bf16[256,768]{1,0:T(8,128)(2,1)}, u32[]{:S(2)}, u32[]{:S(2)}) collective-permute-start(bf16[256,768]{1,0:T(8,128)(2,1)} %pad_maximum_fusion), channel_id=1, source_target_pairs={{0,4},{4,0},{8,12},{12,8},{16,20},{20,16},{24,28},{28,24},{32,36},... | collective-permute-start | bytes 1179656 | tf_op jit(solution)/shard_map/ppermute | solution.py:15
  12.5 2.4 copy-start.19
  19.5 0.7 copy-start.2
  20.2 39.9 %collective-permute-start.3 = (bf16[128,768]{0,1:T(8,128)(2,1)}, bf16[128,768]{0,1:T(8,128)(2,1)}, u32[]{:S(2)}, u32[]{:S(2)}) collective-permute-start(bf16[128,768]{0,1:T(8,128)(2,1)} %pad_maximum_fusion.1), channel_id=1, source_target_pairs={{0,4},{4,0},{8,12},{12,8},{16,20},{20,16},{24,28},{28,24},{32,36},... | collective-permute-start | bytes 589832 | tf_op jit(solution)/shard_map/ppermute | solution.py:15
  26.1 10.1 %collective-permute-start.12 = (bf16[32,768]{1,0:T(8,128)(2,1)}, bf16[32,768]{1,0:T(8,128)(2,1)}, u32[]{:S(2)}, u32[]{:S(2)}) collective-permute-start(bf16[32,768]{1,0:T(8,128)(2,1)} %constant_dynamic-update-slice_fusion.2), channel_id=1, source_target_pairs={{0,4},{4,0},{8,12},{12,8},{16,20},{20,16},{24,28},{28,24},{32,36},... | collective-permute-start | bytes 147464 | tf_op jit(solution)/shard_map/ppermute | solution.py:15
  30.0 30.1 %copy-start.3 = (bf16[128,6,64]{0,2,1:T(8,128)(2,1)S(1)}, bf16[128,6,64]{0,2,1:T(8,128)(2,1)}, u32[]{:S(2)}) copy-start(bf16[128,6,64]{0,2,1:T(8,128)(2,1)} %copy-done.2) | copy-start | bytes 294916
  33.5 30.5 %copy-start.1 = (bf16[512,768]{1,0:T(8,128)(2,1)}, bf16[512,768]{1,0:T(8,128)(2,1)S(1)}, u32[]{:S(2)}) copy-start(bf16[512,768]{1,0:T(8,128)(2,1)S(1)} %maximum_select_fusion.8) | copy-start | bytes 2359300
  33.5 30.5 %collective-permute-start.1 = (bf16[512,768]{1,0:T(8,128)(2,1)S(1)}, bf16[512,768]{1,0:T(8,128)(2,1)}, u32[]{:S(2)}, u32[]{:S(2)}) collective-permute-start(bf16[512,768]{1,0:T(8,128)(2,1)S(1)} %maximum_select_fusion.8), channel_id=1, source_target_pairs={{0,8},{4,12},{8,0},{12,4},{16,24},{20,28},{24,16},{28,20},{32,40},... | collective-permute-start | bytes 2359304 | tf_op jit(solution)/shard_map/ppermute | solution.py:15
  36.0 18.2 %collective-permute-start.7 = (bf16[64,768]{1,0:T(8,128)(2,1)S(1)}, bf16[64,768]{1,0:T(8,128)(2,1)S(1)}, u32[]{:S(2)}, u32[]{:S(2)}) collective-permute-start(bf16[64,768]{1,0:T(8,128)(2,1)S(1)} %constant_dynamic-update-slice_fusion), channel_id=1, source_target_pairs={{0,4},{4,0},{8,12},{12,8},{16,20},{20,16},{24,28},{28,24},{32,36},... | collective-permute-start | bytes 294920 | tf_op jit(solution)/shard_map/ppermute | solution.py:15
  37.1 19.5 %collective-permute-start.13 = (bf16[64,768]{1,0:T(8,128)(2,1)S(1)}, bf16[64,768]{1,0:T(8,128)(2,1)S(1)}, u32[]{:S(2)}, u32[]{:S(2)}) collective-permute-start(bf16[64,768]{1,0:T(8,128)(2,1)S(1)} %maximum_select_fusion.17), channel_id=1, source_target_pairs={{0,8},{4,12},{8,0},{12,4},{16,24},{20,28},{24,16},{28,20},{32,40},... | collective-permute-start | bytes 294920 | tf_op jit(solution)/shard_map/ppermute | solution.py:15
  54.3 9.5 %collective-permute-start.8 = (bf16[128,768]{1,0:T(8,128)(2,1)S(1)}, bf16[128,768]{1,0:T(8,128)(2,1)S(1)}, u32[]{:S(2)}, u32[]{:S(2)}) collective-permute-start(bf16[128,768]{1,0:T(8,128)(2,1)S(1)} %maximum_select_fusion.15), channel_id=1, source_target_pairs={{0,8},{4,12},{8,0},{12,4},{16,24},{20,28},{24,16},{28,20},{32,40},... | collective-permute-start | bytes 589832 | tf_op jit(solution)/shard_map/ppermute | solution.py:15
  56.7 12.0 %collective-permute-start.14 = (bf16[128,768]{1,0:T(8,128)(2,1)S(1)}, bf16[128,768]{1,0:T(8,128)(2,1)S(1)}, u32[]{:S(2)}, u32[]{:S(2)}) collective-permute-start(bf16[128,768]{1,0:T(8,128)(2,1)S(1)} %maximum_select_fusion.16), channel_id=1, source_target_pairs={{0,16},{4,20},{8,24},{12,28},{16,0},{20,4},{24,8},{28,12},{32,48},... | collective-permute-start | bytes 589832 | tf_op jit(solution)/shard_map/ppermute | solution.py:15
  61.2 56.0 %collective-permute-start.4 = (bf16[256,768]{0,1:T(8,128)(2,1)S(1)}, bf16[256,768]{0,1:T(8,128)(2,1)S(1)}, u32[]{:S(2)}, u32[]{:S(2)}) collective-permute-start(bf16[256,768]{0,1:T(8,128)(2,1)S(1)} %maximum_select_fusion.12), channel_id=1, source_target_pairs={{0,8},{4,12},{8,0},{12,4},{16,24},{20,28},{24,16},{28,20},{32,40},... | collective-permute-start | bytes 1179656 | tf_op jit(solution)/shard_map/ppermute | solution.py:15
  63.8 55.0 %collective-permute-start.9 = (bf16[256,768]{1,0:T(8,128)(2,1)S(1)}, bf16[256,768]{1,0:T(8,128)(2,1)S(1)}, u32[]{:S(2)}, u32[]{:S(2)}) collective-permute-start(bf16[256,768]{1,0:T(8,128)(2,1)S(1)} %maximum_select_fusion.13), channel_id=1, source_target_pairs={{0,16},{4,20},{8,24},{12,28},{16,0},{20,4},{24,8},{28,12},{32,48},... | collective-permute-start | bytes 1179656 | tf_op jit(solution)/shard_map/ppermute | solution.py:15
  66.2 259.1 %collective-permute-start.2 = (bf16[1024,768]{1,0:T(8,128)(2,1)S(1)}, bf16[1024,768]{1,0:T(8,128)(2,1)}, u32[]{:S(2)}, u32[]{:S(2)}) collective-permute-start(bf16[1024,768]{1,0:T(8,128)(2,1)S(1)} %maximum_select_fusion.4), channel_id=1, source_target_pairs={{0,16},{4,20},{8,24},{12,28},{16,0},{20,4},{24,8},{28,12},{32,48},... | collective-permute-start | bytes 4718600 | tf_op jit(solution)/shard_map/ppermute | solution.py:15
  68.8 91.7 %collective-permute-start.15 = (bf16[256,768]{1,0:T(8,128)(2,1)S(1)}, bf16[256,768]{1,0:T(8,128)(2,1)}, u32[]{:S(2)}, u32[]{:S(2)}) collective-permute-start(bf16[256,768]{1,0:T(8,128)(2,1)S(1)} %maximum_select_fusion.14), channel_id=1, source_target_pairs={{0,32},{4,36},{8,40},{12,44},{16,48},{20,52},{24,56},{28,60},{32,0... | collective-permute-start | bytes 1179656 | tf_op jit(solution)/shard_map/ppermute | solution.py:15
  118.3 102.3 %collective-permute-start.5 = (bf16[512,768]{0,1:T(8,128)(2,1)}, bf16[512,768]{0,1:T(8,128)(2,1)}, u32[]{:S(2)}, u32[]{:S(2)}) collective-permute-start(bf16[512,768]{0,1:T(8,128)(2,1)} %maximum_select_fusion.9), channel_id=1, source_target_pairs={{0,16},{4,20},{8,24},{12,28},{16,0},{20,4},{24,8},{28,12},{32,48},... | collective-permute-start | bytes 2359304 | tf_op jit(solution)/shard_map/ppermute | solution.py:15
  120.1 194.6 %collective-permute-start.10 = (bf16[512,768]{1,0:T(8,128)(2,1)}, bf16[512,768]{1,0:T(8,128)(2,1)}, u32[]{:S(2)}, u32[]{:S(2)}) collective-permute-start(bf16[512,768]{1,0:T(8,128)(2,1)} %maximum_select_fusion.10), channel_id=1, source_target_pairs={{0,32},{4,36},{8,40},{12,44},{16,48},{20,52},{24,56},{28,60},{32,0... | collective-permute-start | bytes 2359304 | tf_op jit(solution)/shard_map/ppermute | solution.py:15
  162.6 156.8 %collective-permute-start.16 = (bf16[512,768]{1,0:T(8,128)(2,1)}, bf16[512,768]{1,0:T(8,128)(2,1)}, u32[]{:S(2)}, u32[]{:S(2)}) collective-permute-start(bf16[512,768]{1,0:T(8,128)(2,1)} %maximum_select_fusion.11), channel_id=1, source_target_pairs={{0,64},{4,68},{8,72},{12,76},{16,80},{20,84},{24,88},{28,92},{32,9... | collective-permute-start | bytes 2359304 | tf_op jit(solution)/shard_map/ppermute | solution.py:15
  224.2 134.6 %collective-permute-start.6 = (bf16[1024,768]{0,1:T(8,128)(2,1)}, bf16[1024,768]{0,1:T(8,128)(2,1)}, u32[]{:S(2)}, u32[]{:S(2)}) collective-permute-start(bf16[1024,768]{0,1:T(8,128)(2,1)} %maximum_select_fusion.5), channel_id=1, source_target_pairs={{0,32},{4,36},{8,40},{12,44},{16,48},{20,52},{24,56},{28,60},{32,0... | collective-permute-start | bytes 4718600 | tf_op jit(solution)/shard_map/ppermute | solution.py:15
  318.1 67.6 %collective-permute-start.11 = (bf16[1024,768]{1,0:T(8,128)(2,1)}, bf16[1024,768]{1,0:T(8,128)(2,1)}, u32[]{:S(2)}, u32[]{:S(2)}) collective-permute-start(bf16[1024,768]{1,0:T(8,128)(2,1)} %maximum_select_fusion.6), channel_id=1, source_target_pairs={{0,64},{4,68},{8,72},{12,76},{16,80},{20,84},{24,88},{28,92},{32,9... | collective-permute-start | bytes 4718600 | tf_op jit(solution)/shard_map/ppermute | solution.py:15
  322.7 91.4 %collective-permute-start.17 = (bf16[1024,768]{1,0:T(8,128)(2,1)}, bf16[1024,768]{1,0:T(8,128)(2,1)}, u32[]{:S(2)}, u32[]{:S(2)}) collective-permute-start(bf16[1024,768]{1,0:T(8,128)(2,1)} %maximum_select_fusion.7), channel_id=1, source_target_pairs={{0,128},{4,132},{8,136},{12,140},{16,144},{20,148},{24,152},{28,15... | collective-permute-start | bytes 4718600 | tf_op jit(solution)/shard_map/ppermute | solution.py:15
  332.0 1.7 copy-start.7
  358.2 4.8 copy-start.8
  363.0 2.1 copy-start.5
  363.1 2.1 copy-start.17
  365.2 18.3 %copy-start.18 = (pred[2,6]{1,0:T(4,128)(4,1)S(1)}, pred[2,6]{1,0:T(4,128)(4,1)}, u32[]{:S(2)}) copy-start(pred[2,6]{1,0:T(4,128)(4,1)} %get-tuple-element.325) | copy-start | bytes 40
  393.2 1.7 copy-start.4
  393.2 1.7 copy-start.16
  394.8 17.1 %copy-start.20 = (pred[4,6]{0,1:T(8,128)(4,1)S(1)}, pred[4,6]{0,1:T(8,128)(4,1)}, u32[]{:S(2)}) copy-start(pred[4,6]{0,1:T(8,128)(4,1)} %copy.143) | copy-start | bytes 76
  423.1 27.6 %copy-start.15 = (pred[8,6]{0,1:T(8,128)(4,1)S(1)}, pred[8,6]{0,1:T(8,128)(4,1)}, u32[]{:S(2)}) copy-start(pred[8,6]{0,1:T(8,128)(4,1)} %copy.149) | copy-start | bytes 148
  423.1 28.6 %copy-start.9 = (f32[6,256]{1,0:T(8,128)S(1)}, f32[6,256]{1,0:T(8,128)}, u32[]{:S(2)}) copy-start(f32[6,256]{1,0:T(8,128)} %copy-done.8) | copy-start | bytes 18436
  423.1 28.6 %copy-start.10 = (f32[256,6]{0,1:T(8,128)S(1)}, f32[256,6]{0,1:T(8,128)}, u32[]{:S(2)}) copy-start(f32[256,6]{0,1:T(8,128)} %copy.159) | copy-start | bytes 18436
  423.1 28.6 %copy-start.11 = (f32[256,6]{0,1:T(8,128)S(1)}, f32[256,6]{0,1:T(8,128)}, u32[]{:S(2)}) copy-start(f32[256,6]{0,1:T(8,128)} %select_n.341) | copy-start | bytes 18436
  423.1 28.6 %copy-start.12 = (f32[1,256,6]{1,0,2:T(1,128)S(1)}, f32[1,256,6]{1,0,2:T(1,128)}, u32[]{:S(2)}) copy-start(f32[1,256,6]{1,0,2:T(1,128)} %copy.156) | copy-start | bytes 18436
  423.2 28.6 %copy-start.13 = (f32[1,256,6]{1,0,2:T(1,128)S(1)}, f32[1,256,6]{1,0,2:T(1,128)}, u32[]{:S(2)}) copy-start(f32[1,256,6]{1,0,2:T(1,128)} %select_n.343) | copy-start | bytes 18436
  423.2 28.6 %copy-start.14 = (f32[1,256,6]{1,0,2:T(1,128)S(1)}, f32[1,256,6]{1,0,2:T(1,128)}, u32[]{:S(2)}) copy-start(f32[1,256,6]{1,0,2:T(1,128)} %copy.155) | copy-start | bytes 18436
  452.9 1.5 copy-start.6
Sparse Core Ops, SparseCore 0:
  456.5 32.6 reduce-scatter.1
where the time goes:
time: 500 us; the launch traced here: 498 us
  starting transfers between devices  200 us (40%)
  waiting for transfers between devices  101 us (20%)
  matrix products  77.6 us (16%)
  other arithmetic  52.4 us (10%)
  local copies, waits for them, and re-layouts  51.7 us (10%)
  between operations  14.2 us (3%)
    ppermute x18, starting transfers between devices, partner_2(): lax.ppermute(x, axis, [(i, i ^ 1 << distance) for i in range(lax.axis_siz...  200 us
    ppermute x18, waiting for transfers between devices, partner_2(): lax.ppermute(x, axis, [(i, i ^ 1 << distance) for i in range(lax.axis_siz...  68.3 us
    dot_general x24, matrix products, attend(): jnp.dot(probs.astype(jnp.bfloat16), value_set, preferred_element_type=jnp...  38.9 us
    select_n x18, other arithmetic, double_up(): jnp.where(upper == 1, jnp.concatenate([partner, gathered], 0), jnp.concat...  34 us
    reduce_scatter x1, waiting for transfers between devices, local(): lax.psum_scatter(jnp.dot(attention, out_weight, preferred_element_type=jn...  32.8 us
    dot_general x24, matrix products, attend(): jnp.dot(query_set, key_set.T, preferred_element_type=jnp.float32)  32.1 us
    slice x7, local copies, waits for them, and re-layouts, local(): gathered[:, local_width:].reshape(span_rows, local_heads, HDIM)  11.5 us
  transfers between devices with their start and end apart: 19, of which 5 were waited for; matrix products, arithmetic and copies ran while one was open for 27% of the time, Pallas kernels for 0%

commit v1 on v0

v1 whole, which is shorter than its diff:
```python
import jax
import jax.numpy as jnp
from jax import lax
from jax.experimental import pallas as pl
from jax.experimental.pallas import tpu as pltpu
from jax.sharding import PartitionSpec as P

MESH = pl.DeviceIdType.MESH
BF = jnp.bfloat16
F32 = jnp.float32
ROWS = 256
D = 1536
HALF = 128
CH = 64
SCALE = 0.125
LOG2E = 1.4426950408889634
ABSENT = -1e30


def nt(a, b):
    return lax.dot_general(a, b, (((1,), (1,)), ((), ())), preferred_element_type=F32)


def mm(a, b):
    return jnp.dot(a, b, preferred_element_type=F32)


def body(
    tok, w, wout, offs, out,
    T, KV, QQ, ZKV1, ZKV2, ZKV3, ZQ, PQ0, PQ1F, PQ1H, PQ2, PQ3,
    KA, QA, KB, QB, VX, RA, RB, R0, R123, ATT, ATTP, SB1, RB1, SB2, RB2, ACC,
    ts, tr, cs, cr, ls, lr, rs, rr0, rr, ps, pr, s1, r1, s2, r2, loc,
):
    sq = lax.axis_index("seq")
    hd = lax.axis_index("head")
    y = sq // 16
    zh = (sq // 4) % 4
    x = sq % 4
    zl = hd // 2
    core = hd % 2
    par = zh % 2
    p = zh // 2
    fi = 2 * p

    def seq_at(yy, zz, xx):
        return yy * 16 + zz * 4 + xx

    dz = 2 * zl - 1
    g_out = (zh + dz + 4) % 4
    n_out = (seq_at(y, g_out, x), (1 - zl) * 2 + core)
    n_in = (sq, (1 - zl) * 2 + core)
    n_core = (sq, zl * 2 + (1 - core))

    def rcopy(src, dst, ssem, rsem, dev):
        return pltpu.make_async_remote_copy(
            src_ref=src, dst_ref=dst, send_sem=ssem, recv_sem=rsem, device_id=dev, device_id_type=MESH
        )

    def send(src, dst, ssem, rsem, dst_seq):
        @pl.when(dst_seq != sq)
        def _():
            rcopy(src, dst, ssem, rsem, (dst_seq, hd)).start()

        @pl.when(dst_seq == sq)
        def _():
            pltpu.make_async_copy(src, dst, rsem).start()

    def sent(src, dst, ssem, rsem, dst_seq):
        @pl.when(dst_seq != sq)
        def _():
            rcopy(src, dst, ssem, rsem, (dst_seq, hd)).wait_send()

    def arrived(ref, sem):
        pltpu.make_async_copy(ref, ref, sem).wait()

    lo = core * HALF

    def rows_of(sub):
        return pl.ds(pl.multiple_of(lo + sub * CH, CH), CH)

    first, second = 1 - zl, zl
    own_sends = []
    for n, sub in enumerate((first, second)):
        c = rcopy(tok.at[rows_of(sub)], T.at[0, rows_of(sub)], ts.at[n], tr.at[n], n_out)
        c.start()
        own_sends.append(c)

    lane = lax.broadcasted_iota(jnp.int32, (1, 128), 1)
    low = lane < 64

    def targets(h, i):
        o1 = offs[1, 3 * par + h] & 1
        o2 = offs[2, 3 * par + h] & 3
        o3 = offs[3, 3 * par + h] & 7
        t1 = i * 2 + o1
        t2 = (i - 128) * 4 + o2
        t3 = (i - 192) * 8 + o3
        return jnp.where(i < 128, t1, jnp.where(i < 192, t2, jnp.where(i < 224, t3, -1)))

    def sel(h):
        i = lax.broadcasted_iota(jnp.int32, (ROWS, ROWS), 0)
        c = lax.broadcasted_iota(jnp.int32, (ROWS, ROWS), 1)
        return jnp.where(targets(h, i) == c, 1.0, 0.0).astype(BF)

    def sel_t(h, first_row, last_row):
        i = lax.broadcasted_iota(jnp.int32, (ROWS, ROWS), 1)
        c = lax.broadcasted_iota(jnp.int32, (ROWS, ROWS), 0)
        hit = (targets(h, i) == c) & (i >= first_row) & (i < last_row)
        return jnp.where(hit, 1.0, 0.0).astype(BF)

    def role_seq(role, yy):
        return seq_at(yy, zh, (role + 2 * core) % 4)

    x_of = (x + 2 * core) % 4

    def l0_kv(slot_blk, h):
        src = KV.at[slot_blk, h]
        dst = KA.at[pl.ds(pl.multiple_of(x * 512 + (slot_blk % 2) * 256, 256), 256)]
        return src, dst, ls.at[h, slot_blk % 2], lr.at[0], role_seq(h, y)

    def l0_q(h):
        dst = QA.at[pl.ds(pl.multiple_of(x * 256, 256), 256)]
        return PQ0.at[h], dst, ls.at[h, 2], lr.at[1], role_seq(h, y)

    def l1_kv(blk, j):
        dst_ref = (KA, KB)[j]
        dst = dst_ref.at[pl.ds(pl.multiple_of(x * 512 + blk * 128, 128), 128)]
        return ZKV1.at[j, blk], dst, ls.at[3 + j, blk], lr.at[2 * j], role_seq(3, y)

    def l1_q(j):
        if j == 0:
            return PQ1F, QA.at[pl.ds(pl.multiple_of(x * 256, 256), 256)], ls.at[5, 0], lr.at[1], role_seq(3, y)
        return PQ1H, QB.at[pl.ds(pl.multiple_of(x * 128, 128), 128)], ls.at[5, 1], lr.at[3], role_seq(3, y)

    def l2_kv(j):
        si = (y % 2) * 4 + x
        dst = KB.at[pl.ds(pl.multiple_of(si * 256, 256), 256)]
        return ZKV2.at[j // 2], dst, ls.at[6, j], lr.at[2], role_seq(j, y - y % 2)

    def l2_q(j):
        si = (y % 2) * 4 + x
        dst = QB.at[pl.ds(pl.multiple_of(si * 64, 64), 64)]
        return PQ2.at[j], dst, ls.at[7, j], lr.at[3], role_seq(j, y - y % 2)

    def l3_kv(j):
        si = y * 4 + x
        dst = KB.at[pl.ds(pl.multiple_of(si * 128, 128), 128)]
        return ZKV3.at[j // 2], dst, ls.at[8, j], lr.at[2], role_seq(j, 1)

    def l3_q(j):
        si = y * 4 + x
        dst = QB.at[pl.ds(pl.multiple_of(si * 32, 32), 32)]
        return PQ3.at[j], dst, ls.at[9, j], lr.at[3], role_seq(j, 1)

    def project(x_ref, blk):
        xs = x_ref[...]
        for h in range(3):
            yh = mm(xs, w[h]).astype(BF)
            KV[blk, h] = yh[:, :128]
            QQ[blk, h] = yh[:, 128:]

        @pl.when(blk // 2 == p)
        def _():
            for h in range(3):
                send(*l0_kv(blk, h))

        for j in range(2):
            h = fi if j == 0 else 1
            z = mm(sel(h), jnp.concatenate([KV[blk, h], QQ[blk, h]], axis=1)).astype(BF)
            ZKV1[j, blk] = z[0:128, :128]
            ZKV2[j, pl.ds(pl.multiple_of(blk * 64, 64), 64)] = z[128:192, :128]
            ZKV3[j, pl.ds(pl.multiple_of(blk * 32, 32), 32)] = z[192:224, :128]
            ZQ[j, blk] = z[:, 128:]
            send(*l1_kv(blk, j))

    project(tok, zh)

    def fwd(slot_src, slot_dst, sub, n, dev):
        c = rcopy(T.at[slot_src, rows_of(sub)], T.at[slot_dst, rows_of(sub)], ts.at[n], tr.at[n], dev)
        c.start()
        return c

    def share(slot, sub, n):
        c = rcopy(T.at[slot, rows_of(sub)], T.at[slot, rows_of(sub)], cs.at[n], cr.at[n], n_core)
        c.start()
        return c

    def landed(slot, sub, sem):
        arrived(T.at[slot, rows_of(sub)], sem)

    def olo(sub):
        return pl.ds(pl.multiple_of((HALF - lo) + sub * CH, CH), CH)

    def landed_core(slot, sub, sem):
        arrived(T.at[slot, olo(sub)], sem)

    sends = list(own_sends)
    landed(0, zl, tr.at[0])
    sends.append(fwd(0, 1, zl, 2, n_in))
    sends.append(share(0, zl, 0))
    landed(1, 1 - zl, tr.at[2])
    sends.append(fwd(1, 2, 1 - zl, 4, n_out))
    sends.append(share(1, 1 - zl, 2))
    landed(0, 1 - zl, tr.at[1])
    sends.append(fwd(0, 1, 1 - zl, 3, n_in))
    sends.append(share(0, 1 - zl, 1))
    landed_core(0, zl, cr.at[0])
    landed_core(0, 1 - zl, cr.at[1])
    project(T.at[0], g_out)
    landed(2, zl, tr.at[4])
    sends.append(fwd(2, 2, zl, 5, n_in))
    sends.append(share(2, zl, 4))
    landed(1, zl, tr.at[3])
    sends.append(share(1, zl, 3))
    landed_core(1, 1 - zl, cr.at[2])
    landed_core(1, zl, cr.at[3])
    project(T.at[1], (zh - dz + 4) % 4)

    for h in range(3):
        PQ0[h] = jnp.where(low, QQ[2 * p, h], QQ[2 * p + 1, h])
        send(*l0_q(h))

    landed(2, 1 - zl, tr.at[5])
    sends.append(share(2, 1 - zl, 5))
    landed_core(2, zl, cr.at[4])
    landed_core(2, 1 - zl, cr.at[5])
    project(T.at[2], (zh + 2) % 4)

    for t in range(2):
        q = jnp.where(low, ZQ[0, 2 * t], ZQ[0, 2 * t + 1])
        PQ1F[t * 128:(t + 1) * 128] = q[:128]
        PQ2[t] = q[128:192]
        PQ3[t] = q[192:224]
    q = jnp.where(low, ZQ[1, 2 * p], ZQ[1, 2 * p + 1])
    PQ1H[...] = q[:128]
    PQ2[2] = q[128:192]
    PQ3[2] = q[192:224]
    late = [l1_q(0), l1_q(1)]
    for j in range(3):
        late += [l2_kv(j), l2_q(j), l3_kv(j), l3_q(j)]
    for a in late:
        send(*a)

    def attend(Q, K, R, tiles):
        VX[...] = jnp.where(low, jnp.ones((), BF), K[...])

        @pl.loop(0, tiles)
        def _(i):
            r = pl.ds(pl.multiple_of(i * 256, 256), 256)
            q = Q[r]
            qa = jnp.where(low, q, jnp.zeros((), BF))
            qb = jnp.where(low, pltpu.roll(q.astype(F32), 64, 1).astype(BF), jnp.zeros((), BF))
            k = K[...]
            v = VX[...]

            def one(qz):
                s = nt(qz, k)
                m = jnp.max(s, axis=1, keepdims=True)
                e = jnp.exp2((s - m) * (SCALE * LOG2E)).astype(BF)
                return mm(e, v), m

            ua, ma = one(qa)
            ub, mb = one(qb)
            ra = pltpu.roll(ua, 64, 1)
            rb = pltpu.roll(ub, 64, 1)
            tot = jnp.where(low, ua, rb)
            o = jnp.where(low, ra, ub) / tot
            ll = SCALE * jnp.where(low, ma, mb) + jnp.log(tot)
            hi = ll.astype(BF)
            left = ll - hi.astype(F32)
            mid = left.astype(BF)
            tail = (left - mid.astype(F32)).astype(BF)
            l64 = lane & 63
            piece = jnp.where(l64 == 0, hi, jnp.where(l64 == 1, mid, jnp.where(l64 == 2, tail, jnp.zeros((), BF))))
            R[r, 0:128] = o.astype(BF)
            R[r, 128:256] = piece

    arrived(KA, lr.at[0])
    arrived(QA, lr.at[1])
    attend(QA, KA, RA, 4)

    def ret0(xs):
        return (RA.at[pl.ds(pl.multiple_of(xs * 256, 256), 256)], R0.at[x_of], rs.at[xs], rr0.at[x_of], seq_at(y, zh, xs))

    def ret1f(k):
        xs, t = k // 2, k % 2
        return (
            RA.at[pl.ds(pl.multiple_of(xs * 256 + t * 128, 128), 128)],
            R123.at[fi, 0:128],
            rs.at[k],
            rr.at[fi, 0],
            seq_at(y, 2 * t + par, xs),
        )

    def ret1h(xs):
        return (
            RB.at[pl.ds(pl.multiple_of(xs * 128, 128), 128)],
            R123.at[1, 0:128],
            rs.at[8 + xs],
            rr.at[1, 0],
            seq_at(y, zh, xs),
        )

    head_b = jnp.where(x_of == 2, 1, fi)
    zh_b = jnp.where(x_of == 2, zh, 2 * x_of + par)

    def ret2(si):
        return (
            RB.at[pl.ds(pl.multiple_of(si * 64, 64), 64)],
            R123.at[head_b, 128:192],
            rs.at[8 + si],
            rr.at[head_b, 1],
            seq_at(y - y % 2 + si // 4, zh_b, si % 4),
        )

    def ret3(si):
        return (
            RB.at[pl.ds(pl.multiple_of(si * 32, 32), 32)],
            R123.at[head_b, 192:224],
            rs.at[8 + si],
            rr.at[head_b, 2],
            seq_at(si // 4, zh_b, si % 4),
        )

    is_l1 = x_of == 3
    is_l2 = (x_of != 3) & (y % 2 == 0)
    is_l3 = (x_of != 3) & (y == 1)

    def do_all(n, f, act):
        @pl.loop(0, n)
        def _(k):
            act(*f(k))

    @pl.when(x_of != 3)
    def _():
        do_all(4, ret0, send)

    @pl.when(is_l1)
    def _():
        do_all(8, ret1f, send)

    @pl.when(is_l1 | is_l2 | is_l3)
    def _():
        arrived(KB, lr.at[2])
        arrived(QB, lr.at[3])
        attend(QB, KB, RB, 2)

    @pl.when(is_l1)
    def _():
        do_all(4, ret1h, send)

    @pl.when(is_l2)
    def _():
        do_all(8, ret2, send)

    @pl.when(is_l3)
    def _():
        do_all(16, ret3, send)

    R123[:, 224:256] = jnp.zeros((3, 32, 256), BF)
    ji = lax.broadcasted_iota(jnp.int32, (128, 128), 0)
    jo = lax.broadcasted_iota(jnp.int32, (128, 128), 1)
    spread = jnp.where((ji // 64 == jo // 64) & (ji % 64 < 3), 1.0, 0.0).astype(BF)
    row = lax.broadcasted_iota(jnp.int32, (ROWS, 128), 0)
    is_a = par == 0
    lows, highs = [], []
    for h in range(3):
        arrived(R0.at[h], rr0.at[h])
        arrived(R123.at[h, 0:128], rr.at[h, 0])
        arrived(R123.at[h, 128:192], rr.at[h, 1])
        arrived(R123.at[h, 192:224], rr.at[h, 2])
        r0 = R0[h]
        os = [r0[:, :128].astype(F32)]
        logs = [mm(r0[:, 128:], spread)]
        r = R123[h]
        for l, (lo_row, hi_row) in ((1, (0, 128)), (2, (128, 192)), (3, (192, 224))):
            sc = mm(sel_t(h, lo_row, hi_row), r)
            os.append(sc[:, :128])
            lg = mm(sc[:, 128:].astype(BF), spread)
            o_l = offs[l, 3 * par + h] & (2**l - 1)
            logs.append(jnp.where((row & (2**l - 1)) == o_l, lg, ABSENT))
        best = jnp.maximum(jnp.maximum(logs[0], logs[1]), jnp.maximum(logs[2], logs[3]))
        ws = [jnp.exp(v - best) for v in logs]
        den = ws[0] + ws[1] + ws[2] + ws[3]
        num = ws[0] * os[0] + ws[1] * os[1] + ws[2] * os[2] + ws[3] * os[3]
        a = num / den
        ra = pltpu.roll(a, 64, 1)
        lows.append((jnp.where(is_a, a, ra), jnp.where(is_a, ra, a)))
        highs.append((jnp.where(is_a, ra, a), jnp.where(is_a, a, ra)))
    ATT[1, :, 0:128] = jnp.where(low, lows[0][1], highs[1][1]).astype(BF)
    ATT[1, :, 128:256] = lows[2][1].astype(BF)
    partner = (seq_at(y, zh + 1 - 2 * par, x), hd)
    swap = rcopy(ATT.at[1], ATTP, ps, pr, partner)
    swap.start()
    ATT[0, :, 0:128] = jnp.where(low, lows[0][0], highs[1][0]).astype(BF)
    ATT[0, :, 128:256] = lows[2][0].astype(BF)

    mine0 = pl.multiple_of(192 * par, 64)
    other0 = pl.multiple_of(192 * (1 - par), 64)

    def proj(a_ref, start, c):
        cols = slice(c * 512, (c + 1) * 512)
        w01 = wout[pl.ds(start, 128), cols]
        w2 = wout[pl.ds(start + 128, 64), cols]
        return mm(a_ref[:, 0:128], w01) + mm(a_ref[:, 128:192], w2)

    for c in range(3):
        ACC[c] = proj(ATT.at[0], mine0, c)
    swap.wait_recv()
    core_sends = []
    for c in range(3):
        ACC[c] += proj(ATTP, other0, c)
        for zz in range(2):
            SB1[c, zz] = ACC[c, pl.ds(pl.multiple_of(zz * 128 + (1 - core) * 64, 64), 64)].astype(BF)
        cp = rcopy(SB1.at[c], RB1.at[c], s1.at[c], r1.at[c], n_core)
        cp.start()
        core_sends.append(cp)
    in_sends = []
    for c in range(3):
        core_sends[c].wait_recv()
        src = pl.multiple_of((1 - zl) * 128 + core * 64, 64)
        SB2[c] = (ACC[c, pl.ds(src, 64)] + RB1[c, 1 - zl].astype(F32)).astype(BF)
        cp = rcopy(SB2.at[c], RB2.at[c], s2.at[c], r2.at[c], n_in)
        cp.start()
        in_sends.append(cp)
    for c in range(3):
        in_sends[c].wait_recv()
        src = pl.multiple_of(zl * 128 + core * 64, 64)
        tot = ACC[c, pl.ds(src, 64)] + RB1[c, zl].astype(F32) + RB2[c].astype(F32)
        out[:, c * 512:(c + 1) * 512] = tot.astype(BF)

    for c in sends + core_sends + in_sends + [swap]:
        c.wait_send()
    for h in range(3):
        for b in range(2):
            sent(*l0_kv(2 * p + b, h))
        sent(*l0_q(h))
    for j in range(2):
        for blk in range(4):
            sent(*l1_kv(blk, j))
    for a in late:
        sent(*a)

    @pl.when(x_of != 3)
    def _():
        do_all(4, ret0, sent)

    @pl.when(is_l1)
    def _():
        do_all(8, ret1f, sent)
        do_all(4, ret1h, sent)

    @pl.when(is_l2)
    def _():
        do_all(8, ret2, sent)

    @pl.when(is_l3)
    def _():
        do_all(16, ret3, sent)


def local(tokens, query_weight, key_weight, value_weight, offsets, out_weight):
    par = (lax.axis_index("seq") // 4) % 2

    def part(weight):
        return lax.dynamic_slice(weight, (0, 192 * par), (D, 192)).reshape(D, 3, 64)

    q, k, v = part(query_weight), part(key_weight), part(value_weight)
    w = jnp.concatenate([k, v, q, q], axis=2).transpose(1, 0, 2)
    vm = lambda *s: pltpu.VMEM(s, BF)
    dma = lambda *s: pltpu.SemaphoreType.DMA(s)
    return pl.pallas_call(
        body,
        out_shape=jax.ShapeDtypeStruct((64, D), BF),
        in_specs=[pl.BlockSpec(memory_space=pltpu.VMEM)] * 3 + [pl.BlockSpec(memory_space=pltpu.SMEM)],
        out_specs=pl.BlockSpec(memory_space=pltpu.VMEM),
        scratch_shapes=[
            vm(3, 256, D), vm(4, 3, 256, 128), vm(4, 3, 256, 128),
            vm(2, 4, 128, 128), vm(2, 256, 128), vm(2, 128, 128), vm(2, 4, 256, 128),
            vm(3, 256, 128), vm(256, 128), vm(128, 128), vm(3, 64, 128), vm(3, 32, 128),
            vm(2048, 128), vm(1024, 128), vm(2048, 128), vm(512, 128), vm(2048, 128),
            vm(1024, 256), vm(512, 256), vm(3, 256, 256), vm(3, 256, 256),
            vm(2, 256, 256), vm(256, 256), vm(3, 2, 64, 512), vm(3, 2, 64, 512), vm(3, 64, 512), vm(3, 64, 512),
            pltpu.VMEM((3, 256, 512), F32),
            dma(6), dma(6), dma(6), dma(6), dma(10, 4), dma(4), dma(24), dma(3), dma(3, 3), dma(), dma(),
            dma(3), dma(3), dma(3), dma(3), dma(1),
        ],
        compiler_params=pltpu.CompilerParams(has_side_effects=True, vmem_limit_bytes=48 * 1024 * 1024),
    )(tokens, w, out_weight, offsets)


def solution(mesh):
    return jax.shard_map(
        local,
        mesh=mesh,
        in_specs=(
            P("seq", None),
            P(None, "head"),
            P(None, "head"),
            P(None, "head"),
            P(None, "head"),
            P("head", None),
        ),
        out_specs=P(("seq", "head"), None),
        check_vma=False,
    )
```

time: 500 us -> 101 us (0.20)
  starting transfers between devices: 200 us -> 0 us
  waiting for transfers between devices: 101 us -> 0 us
  Pallas kernels: 0 us -> 82.4 us
  matrix products: 77.6 us -> 0 us
  other arithmetic: 52.4 us -> 2.91 us
  local copies, waits for them, and re-layouts: 51.7 us -> 13.8 us
  between operations: 14.2 us -> 0.06 us
    ppermute x18 -> x0, starting transfers between devices: 200 us -> none  [partner_2(): lax.ppermute(x, axis, [(i, i ^ 1 << distance) for i in range(lax.axis_siz...]
    pallas_call x0 -> x1, Pallas kernels: none -> 82.4 us  [local(): pl.pallas_call(body, out_shape=jax.ShapeDtypeStruct((64, D), BF), in_spec...]
    dot_general x52 -> x0, matrix products: 77.6 us -> none  [the longest x24 38.9 us: attend(): jnp.dot(probs.astype(jnp.bfloat16), value_set, preferred_element_type=jnp...]
    ppermute x18 -> x0, waiting for transfers between devices: 68.3 us -> none  [partner_2(): lax.ppermute(x, axis, [(i, i ^ 1 << distance) for i in range(lax.axis_siz...]
    select_n x22 -> x0, other arithmetic: 35 us -> none  [the longest x18 34 us: double_up(): jnp.where(upper == 1, jnp.concatenate([partner, gathered], 0), jnp.concat...]
    reduce_scatter x1 -> x0, waiting for transfers between devices: 32.8 us -> none  [local(): lax.psum_scatter(jnp.dot(attention, out_weight, preferred_element_type=jn...]
    slice x11 -> x0, local copies, waits for them, and re-layouts: 19.5 us -> none  [the longest x7 11.5 us: local(): gathered[:, local_width:].reshape(span_rows, local_heads, HDIM)]
    reduce_sum x28 -> x0, other arithmetic: 11.8 us -> none  [the longest x24 7.36 us: attend(): total = jnp.sum(probs, axis=1)]
  transfers between devices with their start and end apart: 19 -> 0, of which waited for: 5 -> 0; matrix products, arithmetic and copies ran while one was open for 27% -> 0% of each run, Pallas kernels for 0% -> 0%
where the time goes in v1:
time: 101 us; the launch traced here: 99.1 us
  Pallas kernels  82.4 us (82%)
  local copies, waits for them, and re-layouts  13.8 us (14%)
  other arithmetic  2.91 us (3%)
    pallas_call x1, Pallas kernels, local(): pl.pallas_call(body, out_shape=jax.ShapeDtypeStruct((64, D), BF), in_spec...  82.4 us
    unnamed x12, local copies, waits for them, and re-layouts  5.54 us
    reshape x3, local copies, waits for them, and re-layouts, part(): return lax.dynamic_slice(weight, (0, 192 * par), (D, 192)).reshape(D, 3, 64)  4.64 us
    dynamic_slice x2, local copies, waits for them, and re-layouts, part(): return lax.dynamic_slice(weight, (0, 192 * par), (D, 192)).reshape(D, 3, 64)  3.6 us
    transpose x1, other arithmetic, local(): w = jnp.concatenate([k, v, q, q], axis=2).transpose(1, 0, 2)  2.91 us

profile of v1, /device:TPU:1, one launch (start us, length us, event | category | flops | bytes accessed | tf_op | source)
XLA Modules:
  0.0 99.1 jit_solution(2469969792246546546)
XLA Ops:
  0.0 0.0 copy-start
  0.0 1.3 %copy-done = bf16[1536,384]{1,0:T(8,128)(2,1)S(1)} copy-done((bf16[1536,384]{1,0:T(8,128)(2,1)S(1)}, bf16[1536,384]{1,0:T(8,128)(2,1)}, u32[]{:S(2)}) %copy-start) | copy-done | bytes 1179672
  1.3 0.3 constant_dynamic-slice_fusion.2
  1.6 0.3 copy.14
  1.9 0.7 copy.10
  2.6 3.3 %constant_dynamic-slice_fusion = (bf16[1536,192]{1,0:T(8,128)(2,1)S(1)}, bf16[1536,192]{1,0:T(8,128)(2,1)}) fusion(bf16[1536,384]{1,0:T(8,128)(2,1)} %param.7, s32[]{:T(128)S(6)} %select_n.18, bf16[1536,384]{1,0:T(8,128)(2,1)} %param.9), kind=kLoop, calls=%fused_computation.1 | loop fusion | bytes 2359300 | tf_op jit(solution)/shard_map/dynamic_slice | solution.py:466
  5.9 1.1 %copy.16 = bf16[1536,192]{0,1:T(8,128)(2,1)} copy(bf16[1536,192]{1,0:T(8,128)(2,1)S(1)} %get-tuple-element.5) | data formatting | bytes 1179648
  7.0 1.6 %copy.12 = bf16[1536,3,64]{2,0,1:T(8,128)(2,1)S(1)} copy(bf16[1536,3,64]{0,2,1:T(8,128)(2,1)} %bitcast.6) | data formatting | bytes 1179648 | tf_op jit(solution)/shard_map/reshape | solution.py:466
  8.6 2.2 %copy.15 = bf16[1536,192]{0,1:T(8,128)(2,1)} copy(bf16[1536,192]{1,0:T(8,128)(2,1)} %get-tuple-element.6) | data formatting | bytes 1179648
  10.8 2.3 %copy.11 = bf16[1536,3,64]{2,0,1:T(8,128)(2,1)} copy(bf16[1536,3,64]{0,2,1:T(8,128)(2,1)} %bitcast.7) | data formatting | bytes 1179648 | tf_op jit(solution)/shard_map/reshape | solution.py:466
  13.1 0.0 copy-start.1
  13.1 0.0 copy-start.2
  13.1 0.0 copy-start.3
  13.1 2.9 %maximum_bitcast_fusion.w = bf16[3,1536,256]{2,1,0:T(8,128)(2,1)S(1)} fusion(bf16[1536,3,64]{2,0,1:T(8,128)(2,1)S(1)} %copy.12, bf16[1536,3,64]{2,0,1:T(8,128)(2,1)} %copy.11, bf16[1536,3,64]{2,0,1:T(8,128)(2,1)S(1)} %copy.10), kind=kLoop, calls=%fused_computation | loop fusion | flops 9437184 | bytes 4128768 | tf_op jit(solution)/shard_map/transpose | solution.py:469
  16.0 0.0 copy-done.1
  16.0 0.0 copy-done.2
  16.1 0.0 copy-done.3
  16.1 82.4 %shard_map.64 = bf16[64,1536]{1,0:T(8,128)(2,1)S(1)} custom-call(bf16[256,1536]{1,0:T(8,128)(2,1)S(1)} %copy-done.2, bf16[3,1536,256]{2,1,0:T(8,128)(2,1)S(1)} %maximum_bitcast_fusion.w, bf16[384,1536]{1,0:T(8,128)(2,1)S(1)} %copy-done.1, s32[4,6]{1,0:T(4,128)S(1)} %copy-done.3), custom_call_target="tpu_custom_call" | custom-call | tf_op jit(solution)/shard_map/pallas_call | solution.py:472
  98.4 0.7 copy.18
Async XLA Ops:
  0.0 1.3 %copy-start = (bf16[1536,384]{1,0:T(8,128)(2,1)S(1)}, bf16[1536,384]{1,0:T(8,128)(2,1)}, u32[]{:S(2)}) copy-start(bf16[1536,384]{1,0:T(8,128)(2,1)} %param.8) | copy-start | bytes 3538948
  13.1 2.9 %copy-start.1 = (bf16[384,1536]{1,0:T(8,128)(2,1)S(1)}, bf16[384,1536]{1,0:T(8,128)(2,1)}, u32[]{:S(2)}) copy-start(bf16[384,1536]{1,0:T(8,128)(2,1)} %wout.1) | copy-start | bytes 3538948
  13.1 2.9 %copy-start.2 = (bf16[256,1536]{1,0:T(8,128)(2,1)S(1)}, bf16[256,1536]{1,0:T(8,128)(2,1)}, u32[]{:S(2)}) copy-start(bf16[256,1536]{1,0:T(8,128)(2,1)} %tok.1) | copy-start | bytes 2359300
  13.1 2.9 %copy-start.3 = (s32[4,6]{1,0:T(4,128)S(1)}, s32[4,6]{1,0:T(4,128)}, u32[]{:S(2)}) copy-start(s32[4,6]{1,0:T(4,128)} %offs.1) | copy-start | bytes 292

commit v2 on v1

v2 whole, which is shorter than its diff:
```python
import jax
import jax.numpy as jnp
from jax import lax
from jax.experimental import pallas as pl
from jax.experimental.pallas import tpu as pltpu
from jax.sharding import PartitionSpec as P

MESH = pl.DeviceIdType.MESH
BF = jnp.bfloat16
F32 = jnp.float32
ROWS = 256
D = 1536
HALF = 128
CH = 32
SCALE = 0.125
LOG2E = 1.4426950408889634
ABSENT = -1e30


def nt(a, b):
    return lax.dot_general(a, b, (((1,), (1,)), ((), ())), preferred_element_type=F32)


def mm(a, b):
    return jnp.dot(a, b, preferred_element_type=F32)


def body(
    tok, wq, wk, wv, wout, offs, out,
    TOK, WIN, W3, WF, T, KV, QQ, ZKV1, ZKV2, ZKV3, ZQ, PQ0, PQ1F, PQ1H, PQ2, PQ3,
    KA, QA, KB, QB, VX, RA, RB, R0, R123, CA, CR, MS, AT, AF,
    win, ts, tr, cs, cr, ls, lr, rs, rr0, rr, ws, wr, fs, fr,
):
    sq = lax.axis_index("seq")
    hd = lax.axis_index("head")
    y = sq // 16
    zh = (sq // 4) % 4
    x = sq % 4
    zl = hd // 2
    core = hd % 2
    par = zh % 2
    p = zh // 2
    fi = 2 * p

    def seq_at(yy, zz, xx):
        return yy * 16 + zz * 4 + xx

    dz = 2 * zl - 1
    g_out = (zh + dz + 4) % 4
    n_out = (seq_at(y, g_out, x), (1 - zl) * 2 + core)
    n_in = (sq, (1 - zl) * 2 + core)
    n_core = (sq, zl * 2 + (1 - core))

    barrier = pltpu.get_barrier_semaphore()

    def hello(dev):
        pl.semaphore_signal(barrier, inc=1, device_id=dev, device_id_type=MESH)

    hello(n_out)
    hello(n_in)
    hello(n_core)
    hello((sq, (1 - zl) * 2 + (1 - core)))

    @pl.loop(1, 16)
    def _(i):
        j = (y * 4 + x + i) % 16
        hello((seq_at(j // 4, zh, j % 4), hd))

    @pl.loop(0, 4)
    def _(i):
        hello((seq_at(y, zh + 1 - 2 * par, x), i))

    start = pl.multiple_of(128 * par, 128)
    loads = [pltpu.make_async_copy(wsrc.at[:, pl.ds(start, 256)], WIN.at[n], win.at[n]) for n, wsrc in enumerate((wk, wv, wq))]
    own_w = pl.ds(pl.multiple_of(384 * hd, 128), 384)
    load_tok = pltpu.make_async_copy(tok, TOK, win.at[3])
    load_wout = pltpu.make_async_copy(wout, WF.at[own_w], win.at[4])
    load_tok.start()
    for c in loads:
        c.start()
    load_wout.start()

    def rcopy(src, dst, ssem, rsem, dev):
        return pltpu.make_async_remote_copy(
            src_ref=src, dst_ref=dst, send_sem=ssem, recv_sem=rsem, device_id=dev, device_id_type=MESH
        )

    def send(src, dst, ssem, rsem, dst_seq):
        @pl.when(dst_seq != sq)
        def _():
            rcopy(src, dst, ssem, rsem, (dst_seq, hd)).start()

        @pl.when(dst_seq == sq)
        def _():
            pltpu.make_async_copy(src, dst, rsem).start()

    def sent(src, dst, ssem, rsem, dst_seq):
        @pl.when(dst_seq != sq)
        def _():
            rcopy(src, dst, ssem, rsem, (dst_seq, hd)).wait_send()

    def arrived(ref, sem):
        pltpu.make_async_copy(ref, ref, sem).wait()

    lane = lax.broadcasted_iota(jnp.int32, (1, 128), 1)
    low = lane < 64

    lo = core * HALF

    def rows_of(sub, k):
        return pl.ds(pl.multiple_of(lo + sub * 64 + k * CH, CH), CH)

    def olo(sub, k):
        return pl.ds(pl.multiple_of((HALF - lo) + sub * 64 + k * CH, CH), CH)

    load_tok.wait()
    pl.semaphore_wait(barrier, 23)
    sends = []
    for n, (sub, k) in enumerate(((1 - zl, 0), (1 - zl, 1), (zl, 0), (zl, 1))):
        c = rcopy(TOK.at[rows_of(sub, k)], T.at[0, rows_of(sub, k)], ts.at[n], tr.at[n], n_out)
        c.start()
        sends.append(c)

    for c in loads:
        c.wait()

    def mover(rows, with_part):
        r = lax.broadcasted_iota(jnp.int32, (rows, 384), 0)
        c = lax.broadcasted_iota(jnp.int32, (rows, 384), 1)
        src = 64 * par + (c // 128) * 64 + c % 64
        if with_part:
            src = src + ((c // 64) % 2) * 256
        return jnp.where(r == src, 1.0, 0.0).astype(BF)

    pkv = mover(512, True)
    pq = mover(256, False)

    @pl.loop(0, 6)
    def _(i):
        r = pl.ds(pl.multiple_of(i * 256, 256), 256)
        wkv = mm(WIN[0, r], pkv[:256]) + mm(WIN[1, r], pkv[256:])
        wqq = mm(WIN[2, r], pq)
        for h in range(3):
            W3[h, r, 0:128] = wkv[:, h * 128:(h + 1) * 128].astype(BF)
            W3[h, r, 128:256] = wqq[:, h * 128:(h + 1) * 128].astype(BF)

    def targets(h, i):
        o1 = offs[1, 3 * par + h] & 1
        o2 = offs[2, 3 * par + h] & 3
        o3 = offs[3, 3 * par + h] & 7
        t1 = i * 2 + o1
        t2 = (i - 128) * 4 + o2
        t3 = (i - 192) * 8 + o3
        return jnp.where(i < 128, t1, jnp.where(i < 192, t2, jnp.where(i < 224, t3, -1)))

    def sel(h):
        i = lax.broadcasted_iota(jnp.int32, (ROWS, ROWS), 0)
        c = lax.broadcasted_iota(jnp.int32, (ROWS, ROWS), 1)
        return jnp.where(targets(h, i) == c, 1.0, 0.0).astype(BF)

    def sel_t(h, first_row, last_row):
        i = lax.broadcasted_iota(jnp.int32, (ROWS, ROWS), 1)
        c = lax.broadcasted_iota(jnp.int32, (ROWS, ROWS), 0)
        hit = (targets(h, i) == c) & (i >= first_row) & (i < last_row)
        return jnp.where(hit, 1.0, 0.0).astype(BF)

    def role_seq(role, yy):
        return seq_at(yy, zh, (role + 2 * core) % 4)

    x_of = (x + 2 * core) % 4

    def at(ref, first_row, n):
        return ref.at[pl.ds(pl.multiple_of(first_row, n), n)]

    s2 = (y % 2) * 4 + x
    s3 = y * 4 + x
    y2 = y - y % 2

    def l0_kv(blk, h):
        b = blk % 2
        return KV.at[blk, h], at(KA, x * 512 + b * 256, 256), ls.at[h, b], lr.at[0], role_seq(h, y)

    def l0_q(h):
        return PQ0.at[h], at(QA, x * 256, 256), ls.at[h, 2], lr.at[1], role_seq(h, y)

    def l1_kv(blk, j):
        dst = at((KA, KB)[j], x * 512 + blk * 128, 128)
        return ZKV1.at[j, blk], dst, ls.at[3 + j, blk], lr.at[2 * j], role_seq(3, y)

    def l2_kv(blk, j):
        return ZKV2.at[j // 2, blk], at(KB, s2 * 256 + blk * 64, 64), ls.at[5 + j, blk], lr.at[2], role_seq(j, y2)

    def l3_kv(blk, j):
        return ZKV3.at[j // 2, blk], at(KB, s3 * 128 + blk * 32, 32), ls.at[8 + j, blk], lr.at[2], role_seq(j, 1)

    def q_f(t):
        return [
            (PQ1F.at[t], at(QA, x * 256 + t * 128, 128), ls.at[11, t], lr.at[1], role_seq(3, y)),
            (PQ2.at[t], at(QB, s2 * 64, 64), ls.at[12, t], lr.at[3], role_seq(t, y2)),
            (PQ3.at[t], at(QB, s3 * 32, 32), ls.at[13, t], lr.at[3], role_seq(t, 1)),
        ]

    def q_h():
        return [
            (PQ1H, at(QB, x * 128, 128), ls.at[11, 2], lr.at[3], role_seq(3, y)),
            (PQ2.at[2], at(QB, s2 * 64, 64), ls.at[12, 2], lr.at[3], role_seq(2, y2)),
            (PQ3.at[2], at(QB, s3 * 32, 32), ls.at[13, 2], lr.at[3], role_seq(2, 1)),
        ]

    def project(x_ref, blk):
        xs = x_ref[...]
        for h in range(3):
            yh = mm(xs, W3[h]).astype(BF)
            KV[blk, h] = yh[:, :128]
            QQ[blk, h] = yh[:, 128:]

        @pl.when(blk // 2 == p)
        def _():
            for h in range(3):
                send(*l0_kv(blk, h))

        for j in range(2):
            h = fi if j == 0 else 1
            z = mm(sel(h), jnp.concatenate([KV[blk, h], QQ[blk, h]], axis=1)).astype(BF)
            ZKV1[j, blk] = z[0:128, :128]
            ZKV2[j, blk] = z[128:192, :128]
            ZKV3[j, blk] = z[192:224, :128]
            ZQ[j, blk] = z[:, 128:]
            send(*l1_kv(blk, j))
        for j in range(3):
            send(*l2_kv(blk, j))
            send(*l3_kv(blk, j))

    def pack_f(t):
        q = jnp.where(low, ZQ[0, 2 * t], ZQ[0, 2 * t + 1])
        PQ1F[t] = q[:128]
        PQ2[t] = q[128:192]
        PQ3[t] = q[192:224]
        for a in q_f(t):
            send(*a)

    def fwd(src_slot, dst_slot, sub, k, n, dev):
        c = rcopy(T.at[src_slot, rows_of(sub, k)], T.at[dst_slot, rows_of(sub, k)], ts.at[n], tr.at[n], dev)
        c.start()
        sends.append(c)

    def share(slot, sub, k, n):
        c = rcopy(T.at[slot, rows_of(sub, k)], T.at[slot, rows_of(sub, k)], cs.at[n], cr.at[n], n_core)
        c.start()
        sends.append(c)

    def landed(slot, sub, k, sem):
        arrived(T.at[slot, rows_of(sub, k)], sem)

    def shared(slot, sub, k, n):
        arrived(T.at[slot, olo(sub, k)], cr.at[n])

    project(TOK, zh)

    for k in range(2):
        landed(0, zl, k, tr.at[k])
        fwd(0, 1, zl, k, 4 + k, n_in)
        share(0, zl, k, k)
    for k in range(2):
        landed(1, 1 - zl, k, tr.at[4 + k])
        fwd(1, 2, 1 - zl, k, 8 + k, n_out)
        share(1, 1 - zl, k, 4 + k)
    for k in range(2):
        landed(0, 1 - zl, k, tr.at[2 + k])
        fwd(0, 1, 1 - zl, k, 6 + k, n_in)
        share(0, 1 - zl, k, 2 + k)
    for k in range(2):
        shared(0, zl, k, k)
        shared(0, 1 - zl, k, 2 + k)
    project(T.at[0], g_out)
    for k in range(2):
        landed(2, zl, k, tr.at[8 + k])
        fwd(2, 2, zl, k, 10 + k, n_in)
        share(2, zl, k, 8 + k)
    for k in range(2):
        landed(1, zl, k, tr.at[6 + k])
        share(1, zl, k, 6 + k)
    for k in range(2):
        shared(1, 1 - zl, k, 4 + k)
        shared(1, zl, k, 6 + k)
    project(T.at[1], (zh - dz + 4) % 4)

    for h in range(3):
        PQ0[h] = jnp.where(low, QQ[2 * p, h], QQ[2 * p + 1, h])
        send(*l0_q(h))
    q = jnp.where(low, ZQ[1, 2 * p], ZQ[1, 2 * p + 1])
    PQ1H[...] = q[:128]
    PQ2[2] = q[128:192]
    PQ3[2] = q[192:224]
    for a in q_h():
        send(*a)
    pack_f(p)

    def attend(Q, K, R, tiles):
        VX[...] = jnp.where(low, jnp.ones((), BF), K[...])

        @pl.loop(0, tiles)
        def _(i):
            r = pl.ds(pl.multiple_of(i * 256, 256), 256)
            q = Q[r]
            qa = jnp.where(low, q, jnp.zeros((), BF))
            qb = jnp.where(low, pltpu.roll(q.astype(F32), 64, 1).astype(BF), jnp.zeros((), BF))
            k = K[...]
            v = VX[...]

            def one(qz):
                s = nt(qz, k)
                m = jnp.max(s, axis=1, keepdims=True)
                e = jnp.exp2((s - m) * (SCALE * LOG2E)).astype(BF)
                return mm(e, v), m

            ua, ma = one(qa)
            ub, mb = one(qb)
            ra = pltpu.roll(ua, 64, 1)
            rb = pltpu.roll(ub, 64, 1)
            tot = jnp.where(low, ua, rb)
            o = jnp.where(low, ra, ub) / tot
            ll = SCALE * jnp.where(low, ma, mb) + jnp.log(tot)
            hi = ll.astype(BF)
            left = ll - hi.astype(F32)
            mid = left.astype(BF)
            tail = (left - mid.astype(F32)).astype(BF)
            l64 = lane & 63
            piece = jnp.where(l64 == 0, hi, jnp.where(l64 == 1, mid, jnp.where(l64 == 2, tail, jnp.zeros((), BF))))
            R[r, 0:128] = o.astype(BF)
            R[r, 128:256] = piece

    def ret0(xs):
        return at(RA, xs * 256, 256), R0.at[x_of], rs.at[xs], rr0.at[x_of], seq_at(y, zh, xs)

    def ret1f(k):
        xs, t = k // 2, k % 2
        dst = seq_at(y, 2 * t + par, xs)
        return at(RA, xs * 256 + t * 128, 128), R123.at[fi, 0:128], rs.at[k], rr.at[fi, 0], dst

    def ret1h(xs):
        return at(RB, xs * 128, 128), R123.at[1, 0:128], rs.at[8 + xs], rr.at[1, 0], seq_at(y, zh, xs)

    head_b = jnp.where(x_of == 2, 1, fi)
    zh_b = jnp.where(x_of == 2, zh, 2 * x_of + par)

    def ret2(si):
        dst = seq_at(y2 + si // 4, zh_b, si % 4)
        return at(RB, si * 64, 64), R123.at[head_b, 128:192], rs.at[8 + si], rr.at[head_b, 1], dst

    def ret3(si):
        dst = seq_at(si // 4, zh_b, si % 4)
        return at(RB, si * 32, 32), R123.at[head_b, 192:224], rs.at[8 + si], rr.at[head_b, 2], dst

    is_l1 = x_of == 3
    is_l2 = (x_of != 3) & (y % 2 == 0)
    is_l3 = (x_of != 3) & (y == 1)

    def do_all(n, f, act):
        @pl.loop(0, n)
        def _(k):
            act(*f(k))

    @pl.when(x_of != 3)
    def _():
        arrived(KA, lr.at[0])
        arrived(QA, lr.at[1])
        attend(QA, KA, RA, 4)
        do_all(4, ret0, send)

    for k in range(2):
        landed(2, 1 - zl, k, tr.at[10 + k])
        share(2, 1 - zl, k, 10 + k)
    for k in range(2):
        shared(2, zl, k, 8 + k)
        shared(2, 1 - zl, k, 10 + k)
    project(T.at[2], (zh + 2) % 4)
    pack_f(1 - p)

    load_wout.wait()

    def w_rows(first_row, n):
        return WF.at[pl.ds(pl.multiple_of(first_row, 64), n)]

    w_core = rcopy(WF.at[own_w], WF.at[own_w], ws.at[0], wr.at[0], n_core)
    w_in = rcopy(w_rows(384 * hd, 192), w_rows(384 * hd, 192), ws.at[1], wr.at[1], n_in)
    w_out = rcopy(w_rows(384 * hd + 192, 192), w_rows(384 * hd + 192, 192), ws.at[2], wr.at[2], n_out)
    for c in (w_core, w_in, w_out):
        c.start()
        sends.append(c)

    @pl.when(is_l1)
    def _():
        arrived(KA, lr.at[0])
        arrived(QA, lr.at[1])
        attend(QA, KA, RA, 4)
        do_all(8, ret1f, send)

    @pl.when(is_l1 | is_l2 | is_l3)
    def _():
        arrived(KB, lr.at[2])
        arrived(QB, lr.at[3])
        attend(QB, KB, RB, 2)

    @pl.when(is_l1)
    def _():
        do_all(4, ret1h, send)

    @pl.when(is_l2)
    def _():
        do_all(8, ret2, send)

    @pl.when(is_l3)
    def _():
        do_all(16, ret3, send)

    hd_in = (1 - zl) * 2 + core
    arrived(w_rows(384 * hd_in, 192), wr.at[1])
    arrived(w_rows(384 * hd_in + 192, 192), wr.at[2])
    w_pass = rcopy(w_rows(384 * hd_in, 384), w_rows(384 * hd_in, 384), ws.at[3], wr.at[3], n_core)
    w_pass.start()
    sends.append(w_pass)

    R123[:, 224:256] = jnp.zeros((3, 32, 256), BF)
    ji = lax.broadcasted_iota(jnp.int32, (128, 128), 0)
    jo = lax.broadcasted_iota(jnp.int32, (128, 128), 1)
    spread = jnp.where((ji // 64 == jo // 64) & (ji % 64 < 3), 1.0, 0.0).astype(BF)
    row = lax.broadcasted_iota(jnp.int32, (ROWS, 128), 0)
    for h in (1, 0, 2):
        arrived(R0.at[h], rr0.at[h])
        arrived(R123.at[h, 0:128], rr.at[h, 0])
        arrived(R123.at[h, 128:192], rr.at[h, 1])
        arrived(R123.at[h, 192:224], rr.at[h, 2])
        r0 = R0[h]
        os = [r0[:, :128].astype(F32)]
        logs = [mm(r0[:, 128:], spread)]
        r = R123[h]
        for l, (lo_row, hi_row) in ((1, (0, 128)), (2, (128, 192)), (3, (192, 224))):
            sc = mm(sel_t(h, lo_row, hi_row), r)
            os.append(sc[:, :128])
            lg = mm(sc[:, 128:].astype(BF), spread)
            o_l = offs[l, 3 * par + h] & (2**l - 1)
            logs.append(jnp.where((row & (2**l - 1)) == o_l, lg, ABSENT))
        best = jnp.maximum(jnp.maximum(logs[0], logs[1]), jnp.maximum(logs[2], logs[3]))
        wts = [jnp.exp(v - best) for v in logs]
        den = wts[0] + wts[1] + wts[2] + wts[3]
        num = wts[0] * os[0] + wts[1] * os[1] + wts[2] * os[2] + wts[3] * os[3]
        a = num / den
        CA[h] = a
        CR[h] = pltpu.roll(a, 64, 1)

    slot = par * 4 + hd
    for b in range(2):
        LO, HI = (CA, CR) if b == 0 else (CR, CA)
        two = jnp.where(low, LO[par], HI[par + 1])
        lo1, hi1 = LO[2 - 2 * par], HI[2 - 2 * par]
        for i in range(4):
            r = i * 64
            MS[b, i, 0:64] = two[r:r + 64].astype(BF)
            MS[b, i, 64:96] = jnp.where(low, lo1[r:r + 32], hi1[r + 32:r + 64]).astype(BF)

    def final(b, i):
        return MS.at[b, i], AT.at[slot], fs.at[b * 4 + i], fr.at[slot], seq_at(y, 2 * p + b, x), i

    @pl.loop(0, 8)
    def _(n):
        src, dst, ssem, rsem, dseq, dhd = final(n // 4, n % 4)

        @pl.when((dseq != sq) | (dhd != hd))
        def _():
            rcopy(src, dst, ssem, rsem, (dseq, dhd)).start()

        @pl.when((dseq == sq) & (dhd == hd))
        def _():
            pltpu.make_async_copy(src, dst, rsem).start()

    arrived(WF.at[pl.ds(pl.multiple_of(384 * (hd + 1 - 2 * core), 128), 384)], wr.at[0])
    arrived(WF.at[pl.ds(pl.multiple_of(384 * (hd_in + 1 - 2 * core), 128), 384)], wr.at[3])

    for i in range(4):
        arrived(AT.at[i], fr.at[i])
        arrived(AT.at[4 + i], fr.at[4 + i])
        e, o = AT[i], AT[4 + i]
        x0 = e[64:96].astype(F32)
        x1 = o[64:96].astype(F32)
        AF[:, i * 384:i * 384 + 128] = e[:64]
        AF[0:32, i * 384 + 128:i * 384 + 256] = jnp.where(low, x0, pltpu.roll(x1, 64, 1)).astype(BF)
        AF[32:64, i * 384 + 128:i * 384 + 256] = jnp.where(low, pltpu.roll(x0, 64, 1), x1).astype(BF)
        AF[:, i * 384 + 256:(i + 1) * 384] = o[:64]
    out[...] = mm(AF[...], WF[...]).astype(BF)

    for c in sends:
        c.wait_send()

    @pl.loop(0, 8)
    def _(n):
        src, dst, ssem, rsem, dseq, dhd = final(n // 4, n % 4)

        @pl.when((dseq != sq) | (dhd != hd))
        def _():
            rcopy(src, dst, ssem, rsem, (dseq, dhd)).wait_send()

    for h in range(3):
        for b in range(2):
            sent(*l0_kv(2 * p + b, h))
        sent(*l0_q(h))

    @pl.loop(0, 4)
    def _(blk):
        for j in range(2):
            sent(*l1_kv(blk, j))
        for j in range(3):
            sent(*l2_kv(blk, j))
            sent(*l3_kv(blk, j))

    for a in q_h() + q_f(0) + q_f(1):
        sent(*a)

    @pl.when(x_of != 3)
    def _():
        do_all(4, ret0, sent)

    @pl.when(is_l1)
    def _():
        do_all(8, ret1f, sent)
        do_all(4, ret1h, sent)

    @pl.when(is_l2)
    def _():
        do_all(8, ret2, sent)

    @pl.when(is_l3)
    def _():
        do_all(16, ret3, sent)


def local(tokens, query_weight, key_weight, value_weight, offsets, out_weight):
    vm = lambda *s: pltpu.VMEM(s, BF)
    dma = lambda *s: pltpu.SemaphoreType.DMA(s)
    return pl.pallas_call(
        body,
        out_shape=jax.ShapeDtypeStruct((64, D), BF),
        in_specs=[pl.BlockSpec(memory_space=pl.ANY)] * 5 + [pl.BlockSpec(memory_space=pltpu.SMEM)],
        out_specs=pl.BlockSpec(memory_space=pltpu.VMEM),
        scratch_shapes=[
            vm(256, D), vm(3, D, 256), vm(3, D, 256), vm(D, D),
            vm(3, 256, D), vm(4, 3, 256, 128), vm(4, 3, 256, 128),
            vm(2, 4, 128, 128), vm(2, 4, 64, 128), vm(2, 4, 32, 128), vm(2, 4, 256, 128),
            vm(3, 256, 128), vm(2, 128, 128), vm(128, 128), vm(3, 64, 128), vm(3, 32, 128),
            vm(2048, 128), vm(1024, 128), vm(2048, 128), vm(512, 128), vm(2048, 128),
            vm(1024, 256), vm(512, 256), vm(3, 256, 256), vm(3, 256, 256),
            pltpu.VMEM((3, 256, 128), F32), pltpu.VMEM((3, 256, 128), F32),
            vm(2, 4, 96, 128), vm(8, 96, 128), vm(64, D),
            dma(5), dma(12), dma(12), dma(12), dma(12), dma(14, 4), dma(4), dma(24), dma(3), dma(3, 3),
            dma(4), dma(4), dma(8), dma(8),
        ],
        compiler_params=pltpu.CompilerParams(
            has_side_effects=True, collective_id=1, vmem_limit_bytes=48 * 1024 * 1024
        ),
    )(tokens, query_weight, key_weight, value_weight, out_weight, offsets)


def solution(mesh):
    return jax.shard_map(
        local,
        mesh=mesh,
        in_specs=(
            P("seq", None),
            P(None, "head"),
            P(None, "head"),
            P(None, "head"),
            P(None, "head"),
            P("head", None),
        ),
        out_specs=P(("seq", "head"), None),
        check_vma=False,
    )
```

time: 101 us -> 87 us (0.86); the launches traced: 99.1 us -> 86.7 us
  local copies, waits for them, and re-layouts: 13.8 us -> 7.57 us
  Pallas kernels: 82.4 us -> 79.1 us
  other arithmetic: 2.91 us -> 0 us
    reshape x3 -> x0, local copies, waits for them, and re-layouts: 4.64 us -> none  [part(): return lax.dynamic_slice(weight, (0, 192 * par), (D, 192)).reshape(D, 3, 64)]
    dynamic_slice x2 -> x0, local copies, waits for them, and re-layouts: 3.6 us -> none  [part(): return lax.dynamic_slice(weight, (0, 192 * par), (D, 192)).reshape(D, 3, 64)]
    pallas_call x1, Pallas kernels: 82.4 us -> 79.1 us  [local(): pl.pallas_call(body, out_shape=jax.ShapeDtypeStruct((64, D), BF), in_spec...]
    transpose x1 -> x0, other arithmetic: 2.91 us -> none  [local(): w = jnp.concatenate([k, v, q, q], axis=2).transpose(1, 0, 2)]
    unnamed x12 -> x13, local copies, waits for them, and re-layouts: 5.54 us -> 7.57 us
where the time goes in v2:
time: 87 us; the launch traced here: 86.7 us
  Pallas kernels  79.1 us (91%)
  local copies, waits for them, and re-layouts  7.57 us (9%)
    pallas_call x1, Pallas kernels, local(): pl.pallas_call(body, out_shape=jax.ShapeDtypeStruct((64, D), BF), in_spec...  79.1 us
    unnamed x13, local copies, waits for them, and re-layouts  7.57 us

profile of v2, /device:TPU:1, one launch (start us, length us, event | category | flops | bytes accessed | tf_op | source)
XLA Modules:
  0.0 86.7 jit_solution(13823487425009612411)
XLA Ops:
  0.0 0.0 copy-start
  0.0 1.3 %copy-done = bf16[1536,384]{1,0:T(8,128)(2,1)S(1)} copy-done((bf16[1536,384]{1,0:T(8,128)(2,1)S(1)}, bf16[1536,384]{1,0:T(8,128)(2,1)}, u32[]{:S(2)}) %copy-start) | copy-done | bytes 1179672
  1.3 0.0 copy-start.1
  1.3 1.3 %copy-done.1 = bf16[1536,384]{1,0:T(8,128)(2,1)S(1)} copy-done((bf16[1536,384]{1,0:T(8,128)(2,1)S(1)}, bf16[1536,384]{1,0:T(8,128)(2,1)}, u32[]{:S(2)}) %copy-start.1) | copy-done | bytes 1179672
  2.5 0.0 copy-start.2
  2.5 1.3 %copy-done.2 = bf16[1536,384]{1,0:T(8,128)(2,1)S(1)} copy-done((bf16[1536,384]{1,0:T(8,128)(2,1)S(1)}, bf16[1536,384]{1,0:T(8,128)(2,1)}, u32[]{:S(2)}) %copy-start.2) | copy-done | bytes 1179672
  3.8 0.0 copy-start.3
  3.8 1.3 %copy-done.3 = bf16[384,1536]{1,0:T(8,128)(2,1)S(1)} copy-done((bf16[384,1536]{1,0:T(8,128)(2,1)S(1)}, bf16[384,1536]{1,0:T(8,128)(2,1)}, u32[]{:S(2)}) %copy-start.3) | copy-done | bytes 1179672
  5.1 0.0 copy-start.4
  5.1 1.1 %copy-done.4 = bf16[256,1536]{1,0:T(8,128)(2,1)S(1)} copy-done((bf16[256,1536]{1,0:T(8,128)(2,1)S(1)}, bf16[256,1536]{1,0:T(8,128)(2,1)}, u32[]{:S(2)}) %copy-start.4) | copy-done | bytes 786456
  6.2 0.0 copy-start.5
  6.2 0.7 copy-done.5
  6.9 79.1 %shard_map.64 = bf16[64,1536]{1,0:T(8,128)(2,1)S(1)} custom-call(bf16[256,1536]{1,0:T(8,128)(2,1)S(1)} %copy-done.4, bf16[1536,384]{1,0:T(8,128)(2,1)S(1)} %copy-done, bf16[1536,384]{1,0:T(8,128)(2,1)S(1)} %copy-done.1, bf16[1536,384]{1,0:T(8,128)(2,1)S(1)} %copy-done.2, bf16[384,1536]{1,0:T(8,128)(2,1)S(1)} %copy-done.3, s32[4,6]{1,0:T(4,128)S(1)} %copy-done.5), custom_call_target="tpu_custom_call" | custom-call | tf_op jit(solution)/shard_map/pallas_call | solution.py:540
  86.1 0.7 copy.8
Async XLA Ops:
  0.0 1.3 %copy-start = (bf16[1536,384]{1,0:T(8,128)(2,1)S(1)}, bf16[1536,384]{1,0:T(8,128)(2,1)}, u32[]{:S(2)}) copy-start(bf16[1536,384]{1,0:T(8,128)(2,1)} %wq.1) | copy-start | bytes 3538948
  1.3 1.3 %copy-start.1 = (bf16[1536,384]{1,0:T(8,128)(2,1)S(1)}, bf16[1536,384]{1,0:T(8,128)(2,1)}, u32[]{:S(2)}) copy-start(bf16[1536,384]{1,0:T(8,128)(2,1)} %wk.1) | copy-start | bytes 3538948
  2.5 1.3 %copy-start.2 = (bf16[1536,384]{1,0:T(8,128)(2,1)S(1)}, bf16[1536,384]{1,0:T(8,128)(2,1)}, u32[]{:S(2)}) copy-start(bf16[1536,384]{1,0:T(8,128)(2,1)} %wv.1) | copy-start | bytes 3538948
  3.8 1.3 %copy-start.3 = (bf16[384,1536]{1,0:T(8,128)(2,1)S(1)}, bf16[384,1536]{1,0:T(8,128)(2,1)}, u32[]{:S(2)}) copy-start(bf16[384,1536]{1,0:T(8,128)(2,1)} %wout.1) | copy-start | bytes 3538948
  5.1 1.1 %copy-start.4 = (bf16[256,1536]{1,0:T(8,128)(2,1)S(1)}, bf16[256,1536]{1,0:T(8,128)(2,1)}, u32[]{:S(2)}) copy-start(bf16[256,1536]{1,0:T(8,128)(2,1)} %tok.1) | copy-start | bytes 2359300
  6.2 0.7 copy-start.5

commit v3 on v2

--- a/solution.py
+++ b/solution.py
@@ -11,7 +11,6 @@
 ROWS = 256
 D = 1536
 HALF = 128
-CH = 32
 SCALE = 0.125
 LOG2E = 1.4426950408889634
 ABSENT = -1e30
@@ -107,19 +106,26 @@
 
     lo = core * HALF
 
-    def rows_of(sub, k):
-        return pl.ds(pl.multiple_of(lo + sub * 64 + k * CH, CH), CH)
-
-    def olo(sub, k):
-        return pl.ds(pl.multiple_of((HALF - lo) + sub * 64 + k * CH, CH), CH)
+    FAR = [(i * 16, 16) for i in range(4)]
+    NEAR = [(i * 32, 32) for i in range(2)]
+
+    def rows_of(sub, part):
+        return pl.ds(pl.multiple_of(lo + sub * 64 + part[0], part[1]), part[1])
+
+    def other_rows(sub):
+        return pl.ds(pl.multiple_of(HALF - lo + sub * 64, 64), 64)
 
     load_tok.wait()
     pl.semaphore_wait(barrier, 23)
     sends = []
-    for n, (sub, k) in enumerate(((1 - zl, 0), (1 - zl, 1), (zl, 0), (zl, 1))):
-        c = rcopy(TOK.at[rows_of(sub, k)], T.at[0, rows_of(sub, k)], ts.at[n], tr.at[n], n_out)
+
+    def own(sub, part, n):
+        c = rcopy(TOK.at[rows_of(sub, part)], T.at[0, rows_of(sub, part)], ts.at[n], tr.at[n], n_out)
         c.start()
         sends.append(c)
+
+    for k, part in enumerate(FAR):
+        own(1 - zl, part, k)
 
     for c in loads:
         c.wait()
@@ -239,50 +245,51 @@
         for a in q_f(t):
             send(*a)
 
-    def fwd(src_slot, dst_slot, sub, k, n, dev):
-        c = rcopy(T.at[src_slot, rows_of(sub, k)], T.at[dst_slot, rows_of(sub, k)], ts.at[n], tr.at[n], dev)
+    def fwd(src_slot, dst_slot, sub, part, n, dev):
+        c = rcopy(T.at[src_slot, rows_of(sub, part)], T.at[dst_slot, rows_of(sub, part)], ts.at[n], tr.at[n], dev)
         c.start()
         sends.append(c)
 
-    def share(slot, sub, k, n):
-        c = rcopy(T.at[slot, rows_of(sub, k)], T.at[slot, rows_of(sub, k)], cs.at[n], cr.at[n], n_core)
+    def share(slot, sub, n):
+        r = rows_of(sub, (0, 64))
+        c = rcopy(T.at[slot, r], T.at[slot, r], cs.at[n], cr.at[n], n_core)
         c.start()
         sends.append(c)
 
-    def landed(slot, sub, k, sem):
-        arrived(T.at[slot, rows_of(sub, k)], sem)
-
-    def shared(slot, sub, k, n):
-        arrived(T.at[slot, olo(sub, k)], cr.at[n])
+    def landed(slot, sub, part, n):
+        arrived(T.at[slot, rows_of(sub, part)], tr.at[n])
+
+    def shared(slot, sub, n):
+        arrived(T.at[slot, other_rows(sub)], cr.at[n])
 
     project(TOK, zh)
 
-    for k in range(2):
-        landed(0, zl, k, tr.at[k])
-        fwd(0, 1, zl, k, 4 + k, n_in)
-        share(0, zl, k, k)
-    for k in range(2):
-        landed(1, 1 - zl, k, tr.at[4 + k])
-        fwd(1, 2, 1 - zl, k, 8 + k, n_out)
-        share(1, 1 - zl, k, 4 + k)
-    for k in range(2):
-        landed(0, 1 - zl, k, tr.at[2 + k])
-        fwd(0, 1, 1 - zl, k, 6 + k, n_in)
-        share(0, 1 - zl, k, 2 + k)
-    for k in range(2):
-        shared(0, zl, k, k)
-        shared(0, 1 - zl, k, 2 + k)
+    for k, part in enumerate(FAR):
+        landed(0, zl, part, k)
+        fwd(0, 1, zl, part, 6 + k, n_in)
+    for k, part in enumerate(NEAR):
+        own(zl, part, 4 + k)
+    share(0, zl, 0)
+    for k, part in enumerate(FAR):
+        landed(1, 1 - zl, part, 6 + k)
+        fwd(1, 2, 1 - zl, part, 12 + k, n_out)
+    share(1, 1 - zl, 2)
+    for k, part in enumerate(NEAR):
+        landed(0, 1 - zl, part, 4 + k)
+        fwd(0, 1, 1 - zl, part, 10 + k, n_in)
+    share(0, 1 - zl, 1)
+    shared(0, zl, 0)
+    shared(0, 1 - zl, 1)
     project(T.at[0], g_out)
-    for k in range(2):
-        landed(2, zl, k, tr.at[8 + k])
-        fwd(2, 2, zl, k, 10 + k, n_in)
-        share(2, zl, k, 8 + k)
-    for k in range(2):
-        landed(1, zl, k, tr.at[6 + k])
-        share(1, zl, k, 6 + k)
-    for k in range(2):
-        shared(1, 1 - zl, k, 4 + k)
-        shared(1, zl, k, 6 + k)
+    for k, part in enumerate(FAR):
+        landed(2, zl, part, 12 + k)
+        fwd(2, 2, zl, part, 16 + k, n_in)
+    share(2, zl, 4)
+    for k, part in enumerate(NEAR):
+        landed(1, zl, part, 10 + k)
+    share(1, zl, 3)
+    shared(1, 1 - zl, 2)
+    shared(1, zl, 3)
     project(T.at[1], (zh - dz + 4) % 4)
 
     for h in range(3):
@@ -308,14 +315,11 @@
             k = K[...]
             v = VX[...]
 
-            def one(qz):
-                s = nt(qz, k)
-                m = jnp.max(s, axis=1, keepdims=True)
-                e = jnp.exp2((s - m) * (SCALE * LOG2E)).astype(BF)
-                return mm(e, v), m
-
-            ua, ma = one(qa)
-            ub, mb = one(qb)
+            sa, sb = nt(qa, k), nt(qb, k)
+            ma = jnp.max(sa, axis=1, keepdims=True)
+            mb = jnp.max(sb, axis=1, keepdims=True)
+            ua = mm(jnp.exp2((sa - ma) * (SCALE * LOG2E)).astype(BF), v)
+            ub = mm(jnp.exp2((sb - mb) * (SCALE * LOG2E)).astype(BF), v)
             ra = pltpu.roll(ua, 64, 1)
             rb = pltpu.roll(ub, 64, 1)
             tot = jnp.where(low, ua, rb)
@@ -361,19 +365,11 @@
         def _(k):
             act(*f(k))
 
-    @pl.when(x_of != 3)
-    def _():
-        arrived(KA, lr.at[0])
-        arrived(QA, lr.at[1])
-        attend(QA, KA, RA, 4)
-        do_all(4, ret0, send)
-
-    for k in range(2):
-        landed(2, 1 - zl, k, tr.at[10 + k])
-        share(2, 1 - zl, k, 10 + k)
-    for k in range(2):
-        shared(2, zl, k, 8 + k)
-        shared(2, 1 - zl, k, 10 + k)
+    for k, part in enumerate(FAR):
+        landed(2, 1 - zl, part, 16 + k)
+    share(2, 1 - zl, 5)
+    shared(2, zl, 4)
+    shared(2, 1 - zl, 5)
     project(T.at[2], (zh + 2) % 4)
     pack_f(1 - p)
 
@@ -388,6 +384,13 @@
     for c in (w_core, w_in, w_out):
         c.start()
         sends.append(c)
+
+    @pl.when(x_of != 3)
+    def _():
+        arrived(KA, lr.at[0])
+        arrived(QA, lr.at[1])
+        attend(QA, KA, RA, 4)
+        do_all(4, ret0, send)
 
     @pl.when(is_l1)
     def _():
@@ -551,11 +554,11 @@
             vm(1024, 256), vm(512, 256), vm(3, 256, 256), vm(3, 256, 256),
             pltpu.VMEM((3, 256, 128), F32), pltpu.VMEM((3, 256, 128), F32),
             vm(2, 4, 96, 128), vm(8, 96, 128), vm(64, D),
-            dma(5), dma(12), dma(12), dma(12), dma(12), dma(14, 4), dma(4), dma(24), dma(3), dma(3, 3),
+            dma(5), dma(20), dma(20), dma(6), dma(6), dma(14, 4), dma(4), dma(24), dma(3), dma(3, 3),
             dma(4), dma(4), dma(8), dma(8),
         ],
         compiler_params=pltpu.CompilerParams(
-            has_side_effects=True, collective_id=1, vmem_limit_bytes=48 * 1024 * 1024
+            has_side_effects=True, collective_id=1, vmem_limit_bytes=62 * 1024 * 1024
         ),
     )(tokens, query_weight, key_weight, value_weight, out_weight, offsets)
 

time: 87 us -> 70 us (0.80)
  the two profiles are of different devices: /device:TPU:1 before, /device:TPU:239 now
where the time goes in v3:
time: 70 us; the launch traced here: 69.9 us
  Pallas kernels  68.3 us (98%)
  local copies, waits for them, and re-layouts  1.62 us (2%)
    pallas_call x1, Pallas kernels, local(): pl.pallas_call(body, out_shape=jax.ShapeDtypeStruct((64, D), BF), in_spec...  68.3 us
    unnamed x1, local copies, waits for them, and re-layouts  1.62 us

profile of v3, /device:TPU:239, one launch (start us, length us, event | category | flops | bytes accessed | tf_op | source)
XLA Modules:
  0.0 69.9 jit_solution(11399787963546045941)
XLA Ops:
  0.0 68.3 %shard_map.64 = bf16[64,1536]{1,0:T(8,128)(2,1)} custom-call(bf16[256,1536]{1,0:T(8,128)(2,1)} %tok.1, bf16[1536,384]{1,0:T(8,128)(2,1)} %wq.1, bf16[1536,384]{1,0:T(8,128)(2,1)} %wk.1, bf16[1536,384]{1,0:T(8,128)(2,1)} %wv.1, bf16[384,1536]{1,0:T(8,128)(2,1)} %wout.1, s32[4,6]{1,0:T(4,128)} %offs.1), custom_call_target="tpu_custom_call" | custom-call | tf_op jit(solution)/shard_map/pallas_call | solution.py:543
  68.3 1.6 %copy.8 = bf16[64,1536]{1,0:T(8,128)(2,1)} copy(bf16[64,1536]{1,0:T(8,128)(2,1)} %shard_map.64) | data formatting | bytes 393216

commit v4 on v3

--- a/solution.py
+++ b/solution.py
@@ -26,9 +26,10 @@
 
 def body(
     tok, wq, wk, wv, wout, offs, out,
-    TOK, WIN, W3, WF, T, KV, QQ, ZKV1, ZKV2, ZKV3, ZQ, PQ0, PQ1F, PQ1H, PQ2, PQ3,
-    KA, QA, KB, QB, VX, RA, RB, R0, R123, CA, CR, MS, AT, AF,
+    TOK, WIN, W3, WF, T, KV, QQ, ZKV1, ZKV2, ZKV3, ZQ, PQ0, PQ1, PQ2, PQ3,
+    KA, QA, KB, QB, KC, QC, VX, RA, RB, RC, R0, R123, CA, CR, MS, AT, AF,
     win, ts, tr, cs, cr, ls, lr, rs, rr0, rr, ws, wr, fs, fr,
+    sxa, sya, sxb,
 ):
     sq = lax.axis_index("seq")
     hd = lax.axis_index("head")
@@ -39,7 +40,6 @@
     core = hd % 2
     par = zh % 2
     p = zh // 2
-    fi = 2 * p
 
     def seq_at(yy, zz, xx):
         return yy * 16 + zz * 4 + xx
@@ -58,16 +58,14 @@
     hello(n_out)
     hello(n_in)
     hello(n_core)
-    hello((sq, (1 - zl) * 2 + (1 - core)))
-
-    @pl.loop(1, 16)
-    def _(i):
-        j = (y * 4 + x + i) % 16
-        hello((seq_at(j // 4, zh, j % 4), hd))
-
-    @pl.loop(0, 4)
-    def _(i):
-        hello((seq_at(y, zh + 1 - 2 * par, x), i))
+    x_next = [(seq_at(y, zh, (x + d) % 4), hd) for d in (1, 3)]
+    y_next = [(seq_at((y + d) % 4, zh, x), hd) for d in (1, 3)]
+    for dev in x_next + y_next:
+        hello(dev)
+
+    def tell(sem, devs):
+        for dev in devs:
+            pl.semaphore_signal(sem, inc=1, device_id=dev, device_id_type=MESH)
 
     start = pl.multiple_of(128 * par, 128)
     loads = [pltpu.make_async_copy(wsrc.at[:, pl.ds(start, 256)], WIN.at[n], win.at[n]) for n, wsrc in enumerate((wk, wv, wq))]
@@ -116,7 +114,7 @@
         return pl.ds(pl.multiple_of(HALF - lo + sub * 64, 64), 64)
 
     load_tok.wait()
-    pl.semaphore_wait(barrier, 23)
+    pl.semaphore_wait(barrier, 7)
     sends = []
 
     def own(sub, part, n):
@@ -126,6 +124,8 @@
 
     for k, part in enumerate(FAR):
         own(1 - zl, part, k)
+
+    tell(sxa, x_next)
 
     for c in loads:
         c.wait()
@@ -182,35 +182,33 @@
     s3 = y * 4 + x
     y2 = y - y % 2
 
+    L2_AT = ((0, 0), (0, 1), (1, 0))
+    L3_AT = ((3, 1), (3, 3), (2, 0))
+
     def l0_kv(blk, h):
         b = blk % 2
         return KV.at[blk, h], at(KA, x * 512 + b * 256, 256), ls.at[h, b], lr.at[0], role_seq(h, y)
 
-    def l0_q(h):
-        return PQ0.at[h], at(QA, x * 256, 256), ls.at[h, 2], lr.at[1], role_seq(h, y)
-
-    def l1_kv(blk, j):
-        dst = at((KA, KB)[j], x * 512 + blk * 128, 128)
-        return ZKV1.at[j, blk], dst, ls.at[3 + j, blk], lr.at[2 * j], role_seq(3, y)
-
-    def l2_kv(blk, j):
-        return ZKV2.at[j // 2, blk], at(KB, s2 * 256 + blk * 64, 64), ls.at[5 + j, blk], lr.at[2], role_seq(j, y2)
-
-    def l3_kv(blk, j):
-        return ZKV3.at[j // 2, blk], at(KB, s3 * 128 + blk * 32, 32), ls.at[8 + j, blk], lr.at[2], role_seq(j, 1)
-
-    def q_f(t):
+    def l1_kv(blk, h):
+        return ZKV1.at[h, blk], at(KB, x * 512 + blk * 128, 128), ls.at[3 + h, blk], lr.at[2], role_seq(h, y)
+
+    def l2_kv(blk, h):
+        dy, c = L2_AT[h]
+        dst = at((KB, KC)[c], s2 * 256 + blk * 64, 64)
+        return ZKV2.at[h, blk], dst, ls.at[6 + h, blk], lr.at[2 + 2 * c], role_seq(3, y2 + dy)
+
+    def l3_kv(blk, h):
+        role, yy = L3_AT[h]
+        return ZKV3.at[h, blk], at(KC, s3 * 128 + blk * 32, 32), ls.at[9 + h, blk], lr.at[4], role_seq(role, yy)
+
+    def queries(h):
+        dy, c = L2_AT[h]
+        role, yy = L3_AT[h]
         return [
-            (PQ1F.at[t], at(QA, x * 256 + t * 128, 128), ls.at[11, t], lr.at[1], role_seq(3, y)),
-            (PQ2.at[t], at(QB, s2 * 64, 64), ls.at[12, t], lr.at[3], role_seq(t, y2)),
-            (PQ3.at[t], at(QB, s3 * 32, 32), ls.at[13, t], lr.at[3], role_seq(t, 1)),
-        ]
-
-    def q_h():
-        return [
-            (PQ1H, at(QB, x * 128, 128), ls.at[11, 2], lr.at[3], role_seq(3, y)),
-            (PQ2.at[2], at(QB, s2 * 64, 64), ls.at[12, 2], lr.at[3], role_seq(2, y2)),
-            (PQ3.at[2], at(QB, s3 * 32, 32), ls.at[13, 2], lr.at[3], role_seq(2, 1)),
+            (PQ0.at[h], at(QA, x * 256, 256), ls.at[h, 2], lr.at[1], role_seq(h, y)),
+            (PQ1.at[h], at(QB, x * 128, 128), ls.at[12 + h, 0], lr.at[3], role_seq(h, y)),
+            (PQ2.at[h], at((QB, QC)[c], s2 * 64, 64), ls.at[12 + h, 1], lr.at[3 + 2 * c], role_seq(3, y2 + dy)),
+            (PQ3.at[h], at(QC, s3 * 32, 32), ls.at[12 + h, 2], lr.at[5], role_seq(role, yy)),
         ]
 
     def project(x_ref, blk):
@@ -225,25 +223,18 @@
             for h in range(3):
                 send(*l0_kv(blk, h))
 
-        for j in range(2):
-            h = fi if j == 0 else 1
+        for h in range(3):
             z = mm(sel(h), jnp.concatenate([KV[blk, h], QQ[blk, h]], axis=1)).astype(BF)
-            ZKV1[j, blk] = z[0:128, :128]
-            ZKV2[j, blk] = z[128:192, :128]
-            ZKV3[j, blk] = z[192:224, :128]
-            ZQ[j, blk] = z[:, 128:]
-            send(*l1_kv(blk, j))
-        for j in range(3):
-            send(*l2_kv(blk, j))
-            send(*l3_kv(blk, j))
-
-    def pack_f(t):
-        q = jnp.where(low, ZQ[0, 2 * t], ZQ[0, 2 * t + 1])
-        PQ1F[t] = q[:128]
-        PQ2[t] = q[128:192]
-        PQ3[t] = q[192:224]
-        for a in q_f(t):
-            send(*a)
+            ZKV1[h, blk] = z[0:128, :128]
+            ZKV2[h, blk] = z[128:192, :128]
+            ZKV3[h, blk] = z[192:224, :128]
+            ZQ[h, blk] = z[:, 128:]
+            send(*l1_kv(blk, h))
+
+    def far_levels(blk):
+        for h in range(3):
+            send(*l2_kv(blk, h))
+            send(*l3_kv(blk, h))
 
     def fwd(src_slot, dst_slot, sub, part, n, dev):
         c = rcopy(T.at[src_slot, rows_of(sub, part)], T.at[dst_slot, rows_of(sub, part)], ts.at[n], tr.at[n], dev)
@@ -262,7 +253,11 @@
     def shared(slot, sub, n):
         arrived(T.at[slot, other_rows(sub)], cr.at[n])
 
+    pl.semaphore_wait(sxa, 2)
+    tell(sya, y_next)
     project(TOK, zh)
+    pl.semaphore_wait(sya, 2)
+    tell(sxb, x_next)
 
     for k, part in enumerate(FAR):
         landed(0, zl, part, k)
@@ -281,6 +276,9 @@
     shared(0, zl, 0)
     shared(0, 1 - zl, 1)
     project(T.at[0], g_out)
+    pl.semaphore_wait(sxb, 2)
+    far_levels(zh)
+    far_levels(g_out)
     for k, part in enumerate(FAR):
         landed(2, zl, part, 12 + k)
         fwd(2, 2, zl, part, 16 + k, n_in)
@@ -291,24 +289,23 @@
     shared(1, 1 - zl, 2)
     shared(1, zl, 3)
     project(T.at[1], (zh - dz + 4) % 4)
+    far_levels((zh - dz + 4) % 4)
 
     for h in range(3):
         PQ0[h] = jnp.where(low, QQ[2 * p, h], QQ[2 * p + 1, h])
-        send(*l0_q(h))
-    q = jnp.where(low, ZQ[1, 2 * p], ZQ[1, 2 * p + 1])
-    PQ1H[...] = q[:128]
-    PQ2[2] = q[128:192]
-    PQ3[2] = q[192:224]
-    for a in q_h():
-        send(*a)
-    pack_f(p)
+        q = jnp.where(low, ZQ[h, 2 * p], ZQ[h, 2 * p + 1])
+        PQ1[h] = q[:128]
+        PQ2[h] = q[128:192]
+        PQ3[h] = q[192:224]
+        for a in queries(h):
+            send(*a)
 
     def attend(Q, K, R, tiles):
         VX[...] = jnp.where(low, jnp.ones((), BF), K[...])
 
         @pl.loop(0, tiles)
         def _(i):
-            r = pl.ds(pl.multiple_of(i * 256, 256), 256)
+            r = pl.ds(pl.multiple_of(i * 512, 512), 512)
             q = Q[r]
             qa = jnp.where(low, q, jnp.zeros((), BF))
             qb = jnp.where(low, pltpu.roll(q.astype(F32), 64, 1).astype(BF), jnp.zeros((), BF))
@@ -337,28 +334,26 @@
     def ret0(xs):
         return at(RA, xs * 256, 256), R0.at[x_of], rs.at[xs], rr0.at[x_of], seq_at(y, zh, xs)
 
-    def ret1f(k):
-        xs, t = k // 2, k % 2
-        dst = seq_at(y, 2 * t + par, xs)
-        return at(RA, xs * 256 + t * 128, 128), R123.at[fi, 0:128], rs.at[k], rr.at[fi, 0], dst
-
-    def ret1h(xs):
-        return at(RB, xs * 128, 128), R123.at[1, 0:128], rs.at[8 + xs], rr.at[1, 0], seq_at(y, zh, xs)
-
-    head_b = jnp.where(x_of == 2, 1, fi)
-    zh_b = jnp.where(x_of == 2, zh, 2 * x_of + par)
-
-    def ret2(si):
-        dst = seq_at(y2 + si // 4, zh_b, si % 4)
-        return at(RB, si * 64, 64), R123.at[head_b, 128:192], rs.at[8 + si], rr.at[head_b, 1], dst
+    def ret1(xs):
+        return at(RB, xs * 128, 128), R123.at[x_of, 0:128], rs.at[4 + xs], rr.at[x_of, 0], seq_at(y, zh, xs)
+
+    def ret2(R, head, first):
+        def one(si):
+            dst = seq_at(y2 + si // 4, zh, si % 4)
+            return at(R, si * 64, 64), R123.at[head, 128:192], rs.at[first + si], rr.at[head, 1], dst
+
+        return one
+
+    head_3 = jnp.where(x_of == 2, 2, y // 2)
 
     def ret3(si):
-        dst = seq_at(si // 4, zh_b, si % 4)
-        return at(RB, si * 32, 32), R123.at[head_b, 192:224], rs.at[8 + si], rr.at[head_b, 2], dst
-
-    is_l1 = x_of == 3
-    is_l2 = (x_of != 3) & (y % 2 == 0)
-    is_l3 = (x_of != 3) & (y == 1)
+        dst = seq_at(si // 4, zh, si % 4)
+        return at(RC, si * 32, 32), R123.at[head_3, 192:224], rs.at[12 + si], rr.at[head_3, 2], dst
+
+    ret2b = ret2(RB, 2 * (y % 2), 4)
+    ret2c = ret2(RC, 1, 12)
+    is_l2c = (x_of == 3) & (y % 2 == 0)
+    is_l3 = ((x_of == 3) & (y % 2 == 1)) | ((x_of == 2) & (y == 0))
 
     def do_all(n, f, act):
         @pl.loop(0, n)
@@ -371,7 +366,7 @@
     shared(2, zl, 4)
     shared(2, 1 - zl, 5)
     project(T.at[2], (zh + 2) % 4)
-    pack_f(1 - p)
+    far_levels((zh + 2) % 4)
 
     load_wout.wait()
 
@@ -389,29 +384,30 @@
     def _():
         arrived(KA, lr.at[0])
         arrived(QA, lr.at[1])
-        attend(QA, KA, RA, 4)
+        attend(QA, KA, RA, 2)
         do_all(4, ret0, send)
 
-    @pl.when(is_l1)
-    def _():
-        arrived(KA, lr.at[0])
-        arrived(QA, lr.at[1])
-        attend(QA, KA, RA, 4)
-        do_all(8, ret1f, send)
-
-    @pl.when(is_l1 | is_l2 | is_l3)
-    def _():
-        arrived(KB, lr.at[2])
-        arrived(QB, lr.at[3])
-        attend(QB, KB, RB, 2)
-
-    @pl.when(is_l1)
-    def _():
-        do_all(4, ret1h, send)
-
-    @pl.when(is_l2)
-    def _():
-        do_all(8, ret2, send)
+    arrived(KB, lr.at[2])
+    arrived(QB, lr.at[3])
+    attend(QB, KB, RB, 1)
+
+    @pl.when(x_of != 3)
+    def _():
+        do_all(4, ret1, send)
+
+    @pl.when(x_of == 3)
+    def _():
+        do_all(8, ret2b, send)
+
+    @pl.when(is_l2c | is_l3)
+    def _():
+        arrived(KC, lr.at[4])
+        arrived(QC, lr.at[5])
+        attend(QC, KC, RC, 1)
+
+    @pl.when(is_l2c)
+    def _():
+        do_all(8, ret2c, send)
 
     @pl.when(is_l3)
     def _():
@@ -506,31 +502,28 @@
     for h in range(3):
         for b in range(2):
             sent(*l0_kv(2 * p + b, h))
-        sent(*l0_q(h))
+        for a in queries(h):
+            sent(*a)
 
     @pl.loop(0, 4)
     def _(blk):
-        for j in range(2):
-            sent(*l1_kv(blk, j))
-        for j in range(3):
-            sent(*l2_kv(blk, j))
-            sent(*l3_kv(blk, j))
-
-    for a in q_h() + q_f(0) + q_f(1):
-        sent(*a)
+        for h in range(3):
+            sent(*l1_kv(blk, h))
+            sent(*l2_kv(blk, h))
+            sent(*l3_kv(blk, h))
 
     @pl.when(x_of != 3)
     def _():
         do_all(4, ret0, sent)
-
-    @pl.when(is_l1)
-    def _():
-        do_all(8, ret1f, sent)
-        do_all(4, ret1h, sent)
-
-    @pl.when(is_l2)
-    def _():
-        do_all(8, ret2, sent)
+        do_all(4, ret1, sent)
+
+    @pl.when(x_of == 3)
+    def _():
+        do_all(8, ret2b, sent)
+
+    @pl.when(is_l2c)
+    def _():
+        do_all(8, ret2c, sent)
 
     @pl.when(is_l3)
     def _():
@@ -548,14 +541,15 @@
         scratch_shapes=[
             vm(256, D), vm(3, D, 256), vm(3, D, 256), vm(D, D),
             vm(3, 256, D), vm(4, 3, 256, 128), vm(4, 3, 256, 128),
-            vm(2, 4, 128, 128), vm(2, 4, 64, 128), vm(2, 4, 32, 128), vm(2, 4, 256, 128),
-            vm(3, 256, 128), vm(2, 128, 128), vm(128, 128), vm(3, 64, 128), vm(3, 32, 128),
-            vm(2048, 128), vm(1024, 128), vm(2048, 128), vm(512, 128), vm(2048, 128),
-            vm(1024, 256), vm(512, 256), vm(3, 256, 256), vm(3, 256, 256),
+            vm(3, 4, 128, 128), vm(3, 4, 64, 128), vm(3, 4, 32, 128), vm(3, 4, 256, 128),
+            vm(3, 256, 128), vm(3, 128, 128), vm(3, 64, 128), vm(3, 32, 128),
+            vm(2048, 128), vm(1024, 128), vm(2048, 128), vm(512, 128), vm(2048, 128), vm(512, 128), vm(2048, 128),
+            vm(1024, 256), vm(512, 256), vm(512, 256), vm(3, 256, 256), vm(3, 256, 256),
             pltpu.VMEM((3, 256, 128), F32), pltpu.VMEM((3, 256, 128), F32),
             vm(2, 4, 96, 128), vm(8, 96, 128), vm(64, D),
-            dma(5), dma(20), dma(20), dma(6), dma(6), dma(14, 4), dma(4), dma(24), dma(3), dma(3, 3),
+            dma(5), dma(20), dma(20), dma(6), dma(6), dma(15, 4), dma(6), dma(28), dma(3), dma(3, 3),
             dma(4), dma(4), dma(8), dma(8),
+            pltpu.SemaphoreType.REGULAR, pltpu.SemaphoreType.REGULAR, pltpu.SemaphoreType.REGULAR,
         ],
         compiler_params=pltpu.CompilerParams(
             has_side_effects=True, collective_id=1, vmem_limit_bytes=62 * 1024 * 1024

time: 70 us -> 64.3 us (0.919)
  the two profiles are of different devices: /device:TPU:239 before, /device:TPU:1 now
where the time goes in v4:
time: 64.3 us; the launch traced here: 64.2 us
  Pallas kernels  62.5 us (97%)
  local copies, waits for them, and re-layouts  1.62 us (3%)
    pallas_call x1, Pallas kernels, local(): pl.pallas_call(body, out_shape=jax.ShapeDtypeStruct((64, D), BF), in_spec...  62.5 us
    unnamed x1, local copies, waits for them, and re-layouts  1.62 us

profile of v4, /device:TPU:1, one launch (start us, length us, event | category | flops | bytes accessed | tf_op | source)
XLA Modules:
  0.0 64.2 jit_solution(4717122617343806767)
XLA Ops:
  0.0 62.5 %shard_map.64 = bf16[64,1536]{1,0:T(8,128)(2,1)} custom-call(bf16[256,1536]{1,0:T(8,128)(2,1)} %tok.1, bf16[1536,384]{1,0:T(8,128)(2,1)} %wq.1, bf16[1536,384]{1,0:T(8,128)(2,1)} %wk.1, bf16[1536,384]{1,0:T(8,128)(2,1)} %wv.1, bf16[384,1536]{1,0:T(8,128)(2,1)} %wout.1, s32[4,6]{1,0:T(4,128)} %offs.1), custom_call_target="tpu_custom_call" | custom-call | tf_op jit(solution)/shard_map/pallas_call | solution.py:536
  62.6 1.6 %copy.8 = bf16[64,1536]{1,0:T(8,128)(2,1)} copy(bf16[64,1536]{1,0:T(8,128)(2,1)} %shard_map.64) | data formatting | bytes 393216

commit v5 on v4

--- a/solution.py
+++ b/solution.py
@@ -26,8 +26,8 @@
 
 def body(
     tok, wq, wk, wv, wout, offs, out,
-    TOK, WIN, W3, WF, T, KV, QQ, ZKV1, ZKV2, ZKV3, ZQ, PQ0, PQ1, PQ2, PQ3,
-    KA, QA, KB, QB, KC, QC, VX, RA, RB, RC, R0, R123, CA, CR, MS, AT, AF,
+    TOK, WIN, W3, WF, T, KV, ZKV1, ZKV2, ZKV3, PQ0, PQ1, PQ2, PQ3,
+    K, Q, VX, R, R0, R123, CA, CR, MS, AT, AF,
     win, ts, tr, cs, cr, ls, lr, rs, rr0, rr, ws, wr, fs, fr,
     sxa, sya, sxb,
 ):
@@ -124,6 +124,8 @@
 
     for k, part in enumerate(FAR):
         own(1 - zl, part, k)
+    for k, part in enumerate(NEAR):
+        own(zl, part, 4 + k)
 
     tell(sxa, x_next)
 
@@ -167,7 +169,11 @@
     def sel_t(h, first_row, last_row):
         i = lax.broadcasted_iota(jnp.int32, (ROWS, ROWS), 1)
         c = lax.broadcasted_iota(jnp.int32, (ROWS, ROWS), 0)
-        hit = (targets(h, i) == c) & (i >= first_row) & (i < last_row)
+        level = {0: 1, 128: 2, 192: 3}[first_row]
+        n = (last_row - first_row) // 2
+        j = i - first_row
+        o = offs[level, 3 * par + h] & (2**level - 1)
+        hit = ((j // n) * 128 + (j % n) * 2**level + o == c) & (i >= first_row) & (i < last_row)
         return jnp.where(hit, 1.0, 0.0).astype(BF)
 
     def role_seq(role, yy):
@@ -182,59 +188,82 @@
     s3 = y * 4 + x
     y2 = y - y % 2
 
-    L2_AT = ((0, 0), (0, 1), (1, 0))
+    L2_AT = ((3, 0, 1), (3, 0, 2), (3, 1, 1))
     L3_AT = ((3, 1), (3, 3), (2, 0))
 
     def l0_kv(blk, h):
         b = blk % 2
-        return KV.at[blk, h], at(KA, x * 512 + b * 256, 256), ls.at[h, b], lr.at[0], role_seq(h, y)
+        return KV.at[blk, h], at(K.at[0], x * 512 + b * 256, 256), ls.at[h, b], lr.at[0], role_seq(h, y)
 
     def l1_kv(blk, h):
-        return ZKV1.at[h, blk], at(KB, x * 512 + blk * 128, 128), ls.at[3 + h, blk], lr.at[2], role_seq(h, y)
+        return ZKV1.at[h, blk], at(K.at[1], x * 512 + blk * 128, 128), ls.at[3 + h, blk], lr.at[2], role_seq(h, y)
 
     def l2_kv(blk, h):
-        dy, c = L2_AT[h]
-        dst = at((KB, KC)[c], s2 * 256 + blk * 64, 64)
-        return ZKV2.at[h, blk], dst, ls.at[6 + h, blk], lr.at[2 + 2 * c], role_seq(3, y2 + dy)
+        role, dy, c = L2_AT[h]
+        dst = at(K.at[c], s2 * 256 + blk * 64, 64)
+        return ZKV2.at[h, blk], dst, ls.at[6 + h, blk], lr.at[2 * c], role_seq(role, y2 + dy)
 
     def l3_kv(blk, h):
         role, yy = L3_AT[h]
-        return ZKV3.at[h, blk], at(KC, s3 * 128 + blk * 32, 32), ls.at[9 + h, blk], lr.at[4], role_seq(role, yy)
-
-    def queries(h):
-        dy, c = L2_AT[h]
-        role, yy = L3_AT[h]
+        return ZKV3.at[h, blk], at(K.at[2], s3 * 128 + blk * 32, 32), ls.at[9 + h, blk], lr.at[4], role_seq(role, yy)
+
+    def near_queries(blk, h):
+        b = blk % 2
         return [
-            (PQ0.at[h], at(QA, x * 256, 256), ls.at[h, 2], lr.at[1], role_seq(h, y)),
-            (PQ1.at[h], at(QB, x * 128, 128), ls.at[12 + h, 0], lr.at[3], role_seq(h, y)),
-            (PQ2.at[h], at((QB, QC)[c], s2 * 64, 64), ls.at[12 + h, 1], lr.at[3 + 2 * c], role_seq(3, y2 + dy)),
-            (PQ3.at[h], at(QC, s3 * 32, 32), ls.at[12 + h, 2], lr.at[5], role_seq(role, yy)),
+            (PQ0.at[h, b], at(Q.at[x // 2], (x % 2) * 256 + b * 128, 128), ls.at[12 + h, b], lr.at[1], role_seq(h, y)),
+            (PQ1.at[h, b], at(Q.at[2], x * 128 + b * 64, 64), ls.at[12 + h, 2 + b], lr.at[3], role_seq(h, y)),
         ]
+
+    def far_queries(blk, h):
+        b = blk % 2
+        r2, dy, c = L2_AT[h]
+        r3, yy = L3_AT[h]
+        dst = at(Q.at[c + 1], s2 * 64 + b * 32, 32)
+        return [
+            (PQ2.at[h, b], dst, ls.at[15 + h, b], lr.at[2 * c + 1], role_seq(r2, y2 + dy)),
+            (PQ3.at[h, b], at(Q.at[3], s3 * 32 + b * 16, 16), ls.at[15 + h, 2 + b], lr.at[5], role_seq(r3, yy)),
+        ]
+
+    def project_head(xs, blk, h):
+        own_pair = blk // 2 == p
+        yh = mm(xs, W3[h]).astype(BF)
+        KV[blk, h] = yh[:, :128]
+
+        @pl.when(own_pair)
+        def _():
+            PQ0[h, blk % 2] = jnp.where(low, yh[:128, 128:], yh[128:, 128:])
+            send(*l0_kv(blk, h))
+
+        z = mm(sel(h), yh).astype(BF)
+        ZKV1[h, blk] = z[0:128, :128]
+        ZKV2[h, blk] = z[128:192, :128]
+        ZKV3[h, blk] = z[192:224, :128]
+        send(*l1_kv(blk, h))
+
+        @pl.when(own_pair)
+        def _():
+            b = blk % 2
+            PQ1[h, b] = jnp.where(low, z[0:64, 128:], z[64:128, 128:])
+            PQ2[h, b] = jnp.where(low, z[128:160, 128:], z[160:192, 128:])
+            PQ3[h, b] = jnp.where(low, z[192:208, 128:], z[208:224, 128:])
+            for a in near_queries(blk, h):
+                send(*a)
 
     def project(x_ref, blk):
         xs = x_ref[...]
         for h in range(3):
-            yh = mm(xs, W3[h]).astype(BF)
-            KV[blk, h] = yh[:, :128]
-            QQ[blk, h] = yh[:, 128:]
-
-        @pl.when(blk // 2 == p)
-        def _():
-            for h in range(3):
-                send(*l0_kv(blk, h))
-
-        for h in range(3):
-            z = mm(sel(h), jnp.concatenate([KV[blk, h], QQ[blk, h]], axis=1)).astype(BF)
-            ZKV1[h, blk] = z[0:128, :128]
-            ZKV2[h, blk] = z[128:192, :128]
-            ZKV3[h, blk] = z[192:224, :128]
-            ZQ[h, blk] = z[:, 128:]
-            send(*l1_kv(blk, h))
+            project_head(xs, blk, h)
 
     def far_levels(blk):
         for h in range(3):
             send(*l2_kv(blk, h))
             send(*l3_kv(blk, h))
+
+        @pl.when(blk // 2 == p)
+        def _():
+            for h in range(3):
+                for a in far_queries(blk, h):
+                    send(*a)
 
     def fwd(src_slot, dst_slot, sub, part, n, dev):
         c = rcopy(T.at[src_slot, rows_of(sub, part)], T.at[dst_slot, rows_of(sub, part)], ts.at[n], tr.at[n], dev)
@@ -253,36 +282,34 @@
     def shared(slot, sub, n):
         arrived(T.at[slot, other_rows(sub)], cr.at[n])
 
+    for k, part in enumerate(FAR):
+        landed(0, zl, part, k)
+        fwd(0, 1, zl, part, 6 + k, n_in)
+    share(0, zl, 0)
     pl.semaphore_wait(sxa, 2)
     tell(sya, y_next)
     project(TOK, zh)
     pl.semaphore_wait(sya, 2)
     tell(sxb, x_next)
-
-    for k, part in enumerate(FAR):
-        landed(0, zl, part, k)
-        fwd(0, 1, zl, part, 6 + k, n_in)
     for k, part in enumerate(NEAR):
-        own(zl, part, 4 + k)
-    share(0, zl, 0)
+        landed(0, 1 - zl, part, 4 + k)
+        fwd(0, 1, 1 - zl, part, 10 + k, n_in)
+    share(0, 1 - zl, 1)
     for k, part in enumerate(FAR):
         landed(1, 1 - zl, part, 6 + k)
         fwd(1, 2, 1 - zl, part, 12 + k, n_out)
     share(1, 1 - zl, 2)
-    for k, part in enumerate(NEAR):
-        landed(0, 1 - zl, part, 4 + k)
-        fwd(0, 1, 1 - zl, part, 10 + k, n_in)
-    share(0, 1 - zl, 1)
+    pl.semaphore_wait(sxb, 2)
+    far_levels(zh)
     shared(0, zl, 0)
     shared(0, 1 - zl, 1)
-    project(T.at[0], g_out)
-    pl.semaphore_wait(sxb, 2)
-    far_levels(zh)
-    far_levels(g_out)
     for k, part in enumerate(FAR):
+        if k < 3:
+            project_head(T[0], g_out, k)
         landed(2, zl, part, 12 + k)
         fwd(2, 2, zl, part, 16 + k, n_in)
     share(2, zl, 4)
+    far_levels(g_out)
     for k, part in enumerate(NEAR):
         landed(1, zl, part, 10 + k)
     share(1, zl, 3)
@@ -291,56 +318,45 @@
     project(T.at[1], (zh - dz + 4) % 4)
     far_levels((zh - dz + 4) % 4)
 
-    for h in range(3):
-        PQ0[h] = jnp.where(low, QQ[2 * p, h], QQ[2 * p + 1, h])
-        q = jnp.where(low, ZQ[h, 2 * p], ZQ[h, 2 * p + 1])
-        PQ1[h] = q[:128]
-        PQ2[h] = q[128:192]
-        PQ3[h] = q[192:224]
-        for a in queries(h):
-            send(*a)
-
-    def attend(Q, K, R, tiles):
-        VX[...] = jnp.where(low, jnp.ones((), BF), K[...])
-
-        @pl.loop(0, tiles)
-        def _(i):
-            r = pl.ds(pl.multiple_of(i * 512, 512), 512)
-            q = Q[r]
-            qa = jnp.where(low, q, jnp.zeros((), BF))
-            qb = jnp.where(low, pltpu.roll(q.astype(F32), 64, 1).astype(BF), jnp.zeros((), BF))
-            k = K[...]
-            v = VX[...]
-
-            sa, sb = nt(qa, k), nt(qb, k)
-            ma = jnp.max(sa, axis=1, keepdims=True)
-            mb = jnp.max(sb, axis=1, keepdims=True)
-            ua = mm(jnp.exp2((sa - ma) * (SCALE * LOG2E)).astype(BF), v)
-            ub = mm(jnp.exp2((sb - mb) * (SCALE * LOG2E)).astype(BF), v)
-            ra = pltpu.roll(ua, 64, 1)
-            rb = pltpu.roll(ub, 64, 1)
-            tot = jnp.where(low, ua, rb)
-            o = jnp.where(low, ra, ub) / tot
-            ll = SCALE * jnp.where(low, ma, mb) + jnp.log(tot)
-            hi = ll.astype(BF)
-            left = ll - hi.astype(F32)
-            mid = left.astype(BF)
-            tail = (left - mid.astype(F32)).astype(BF)
-            l64 = lane & 63
-            piece = jnp.where(l64 == 0, hi, jnp.where(l64 == 1, mid, jnp.where(l64 == 2, tail, jnp.zeros((), BF))))
-            R[r, 0:128] = o.astype(BF)
-            R[r, 128:256] = piece
+    def attend(t):
+        job = jnp.maximum(t - 1, 0)
+        VX[...] = jnp.where(low, jnp.ones((), BF), K[job])
+        q = Q[t]
+        qa = jnp.where(low, q, jnp.zeros((), BF))
+        qb = jnp.where(low, pltpu.roll(q.astype(F32), 64, 1).astype(BF), jnp.zeros((), BF))
+        k = K[job]
+        v = VX[...]
+
+        sa, sb = nt(qa, k), nt(qb, k)
+        ma = jnp.max(sa, axis=1, keepdims=True)
+        mb = jnp.max(sb, axis=1, keepdims=True)
+        ua = mm(jnp.exp2((sa - ma) * (SCALE * LOG2E)).astype(BF), v)
+        ub = mm(jnp.exp2((sb - mb) * (SCALE * LOG2E)).astype(BF), v)
+        ra = pltpu.roll(ua, 64, 1)
+        rb = pltpu.roll(ub, 64, 1)
+        tot = jnp.where(low, ua, rb)
+        o = jnp.where(low, ra, ub) / tot
+        ll = SCALE * jnp.where(low, ma, mb) + jnp.log(tot)
+        hi = ll.astype(BF)
+        left = ll - hi.astype(F32)
+        mid = left.astype(BF)
+        tail = (left - mid.astype(F32)).astype(BF)
+        l64 = lane & 63
+        piece = jnp.where(l64 == 0, hi, jnp.where(l64 == 1, mid, jnp.where(l64 == 2, tail, jnp.zeros((), BF))))
+        R[t, :, 0:128] = o.astype(BF)
+        R[t, :, 128:256] = piece
 
     def ret0(xs):
-        return at(RA, xs * 256, 256), R0.at[x_of], rs.at[xs], rr0.at[x_of], seq_at(y, zh, xs)
+        src = at(R.at[xs // 2], (xs % 2) * 256, 256)
+        return src, R0.at[x_of], rs.at[xs], rr0.at[x_of], seq_at(y, zh, xs)
 
     def ret1(xs):
-        return at(RB, xs * 128, 128), R123.at[x_of, 0:128], rs.at[4 + xs], rr.at[x_of, 0], seq_at(y, zh, xs)
-
-    def ret2(R, head, first):
+        return at(R.at[2], xs * 128, 128), R123.at[x_of, 0:128], rs.at[4 + xs], rr.at[x_of, 0], seq_at(y, zh, xs)
+
+    def ret2(tile, head, first):
         def one(si):
             dst = seq_at(y2 + si // 4, zh, si % 4)
-            return at(R, si * 64, 64), R123.at[head, 128:192], rs.at[first + si], rr.at[head, 1], dst
+            return at(R.at[tile], si * 64, 64), R123.at[head, 128:192], rs.at[first + si], rr.at[head, 1], dst
 
         return one
 
@@ -348,10 +364,10 @@
 
     def ret3(si):
         dst = seq_at(si // 4, zh, si % 4)
-        return at(RC, si * 32, 32), R123.at[head_3, 192:224], rs.at[12 + si], rr.at[head_3, 2], dst
-
-    ret2b = ret2(RB, 2 * (y % 2), 4)
-    ret2c = ret2(RC, 1, 12)
+        return at(R.at[3], si * 32, 32), R123.at[head_3, 192:224], rs.at[12 + si], rr.at[head_3, 2], dst
+
+    ret2b = ret2(2, 2 * (y % 2), 4)
+    ret2c = ret2(3, 1, 12)
     is_l2c = (x_of == 3) & (y % 2 == 0)
     is_l3 = ((x_of == 3) & (y % 2 == 1)) | ((x_of == 2) & (y == 0))
 
@@ -380,38 +396,43 @@
         c.start()
         sends.append(c)
 
-    @pl.when(x_of != 3)
-    def _():
-        arrived(KA, lr.at[0])
-        arrived(QA, lr.at[1])
-        attend(QA, KA, RA, 2)
-        do_all(4, ret0, send)
-
-    arrived(KB, lr.at[2])
-    arrived(QB, lr.at[3])
-    attend(QB, KB, RB, 1)
-
-    @pl.when(x_of != 3)
-    def _():
-        do_all(4, ret1, send)
-
-    @pl.when(x_of == 3)
-    def _():
-        do_all(8, ret2b, send)
-
-    @pl.when(is_l2c | is_l3)
-    def _():
-        arrived(KC, lr.at[4])
-        arrived(QC, lr.at[5])
-        attend(QC, KC, RC, 1)
-
-    @pl.when(is_l2c)
-    def _():
-        do_all(8, ret2c, send)
-
-    @pl.when(is_l3)
-    def _():
-        do_all(16, ret3, send)
+    first = jnp.where(x_of == 3, 2, 0)
+    last = jnp.where(is_l2c | is_l3, 4, 3)
+
+    @pl.loop(first, last)
+    def _(t):
+        for n, first_tile in enumerate((0, 2, 3)):
+
+            @pl.when(t == first_tile)
+            def _():
+                arrived(K.at[n], lr.at[2 * n])
+                if n == 0:
+                    arrived(Q.at[0:2], lr.at[1])
+                else:
+                    arrived(Q.at[n + 1], lr.at[2 * n + 1])
+
+        attend(t)
+
+        @pl.when(t < 2)
+        def _():
+            send(*ret0(2 * t))
+            send(*ret0(2 * t + 1))
+
+        @pl.when((t == 2) & (x_of != 3))
+        def _():
+            do_all(4, ret1, send)
+
+        @pl.when((t == 2) & (x_of == 3))
+        def _():
+            do_all(8, ret2b, send)
+
+        @pl.when((t == 3) & is_l2c)
+        def _():
+            do_all(8, ret2c, send)
+
+        @pl.when((t == 3) & is_l3)
+        def _():
+            do_all(16, ret3, send)
 
     hd_in = (1 - zl) * 2 + core
     arrived(w_rows(384 * hd_in, 192), wr.at[1])
@@ -449,12 +470,12 @@
         CR[h] = pltpu.roll(a, 64, 1)
 
     slot = par * 4 + hd
-    for b in range(2):
-        LO, HI = (CA, CR) if b == 0 else (CR, CA)
+    for i in range(4):
+        LO, HI = (CA, CR) if i < 2 else (CR, CA)
         two = jnp.where(low, LO[par], HI[par + 1])
         lo1, hi1 = LO[2 - 2 * par], HI[2 - 2 * par]
-        for i in range(4):
-            r = i * 64
+        for b in range(2):
+            r = b * 128 + (i % 2) * 64
             MS[b, i, 0:64] = two[r:r + 64].astype(BF)
             MS[b, i, 64:96] = jnp.where(low, lo1[r:r + 32], hi1[r + 32:r + 64]).astype(BF)
 
@@ -502,8 +523,8 @@
     for h in range(3):
         for b in range(2):
             sent(*l0_kv(2 * p + b, h))
-        for a in queries(h):
-            sent(*a)
+            for a in near_queries(2 * p + b, h) + far_queries(2 * p + b, h):
+                sent(*a)
 
     @pl.loop(0, 4)
     def _(blk):
@@ -540,14 +561,13 @@
         out_specs=pl.BlockSpec(memory_space=pltpu.VMEM),
         scratch_shapes=[
             vm(256, D), vm(3, D, 256), vm(3, D, 256), vm(D, D),
-            vm(3, 256, D), vm(4, 3, 256, 128), vm(4, 3, 256, 128),
-            vm(3, 4, 128, 128), vm(3, 4, 64, 128), vm(3, 4, 32, 128), vm(3, 4, 256, 128),
-            vm(3, 256, 128), vm(3, 128, 128), vm(3, 64, 128), vm(3, 32, 128),
-            vm(2048, 128), vm(1024, 128), vm(2048, 128), vm(512, 128), vm(2048, 128), vm(512, 128), vm(2048, 128),
-            vm(1024, 256), vm(512, 256), vm(512, 256), vm(3, 256, 256), vm(3, 256, 256),
+            vm(3, 256, D), vm(4, 3, 256, 128),
+            vm(3, 4, 128, 128), vm(3, 4, 64, 128), vm(3, 4, 32, 128),
+            vm(3, 2, 128, 128), vm(3, 2, 64, 128), vm(3, 2, 32, 128), vm(3, 2, 16, 128),
+            vm(3, 2048, 128), vm(4, 512, 128), vm(2048, 128), vm(4, 512, 256), vm(3, 256, 256), vm(3, 256, 256),
             pltpu.VMEM((3, 256, 128), F32), pltpu.VMEM((3, 256, 128), F32),
             vm(2, 4, 96, 128), vm(8, 96, 128), vm(64, D),
-            dma(5), dma(20), dma(20), dma(6), dma(6), dma(15, 4), dma(6), dma(28), dma(3), dma(3, 3),
+            dma(5), dma(20), dma(20), dma(6), dma(6), dma(18, 4), dma(6), dma(28), dma(3), dma(3, 3),
             dma(4), dma(4), dma(8), dma(8),
             pltpu.SemaphoreType.REGULAR, pltpu.SemaphoreType.REGULAR, pltpu.SemaphoreType.REGULAR,
         ],

time: 64.3 us -> 61.5 us (0.956)
  Pallas kernels: 62.5 us -> 59.7 us
    pallas_call x1, Pallas kernels: 62.5 us -> 59.7 us  [local(): pl.pallas_call(body, out_shape=jax.ShapeDtypeStruct((64, D), BF), in_spec...]
where the time goes in v5:
time: 61.5 us; the launch traced here: 61.4 us
  Pallas kernels  59.7 us (97%)
  local copies, waits for them, and re-layouts  1.62 us (3%)
    pallas_call x1, Pallas kernels, local(): pl.pallas_call(body, out_shape=jax.ShapeDtypeStruct((64, D), BF), in_spec...  59.7 us
    unnamed x1, local copies, waits for them, and re-layouts  1.62 us

profile of v5, /device:TPU:1, one launch (start us, length us, event | category | flops | bytes accessed | tf_op | source)
XLA Modules:
  0.0 61.4 jit_solution(6316311359540265290)
XLA Ops:
  0.0 59.7 %shard_map.64 = bf16[64,1536]{1,0:T(8,128)(2,1)} custom-call(bf16[256,1536]{1,0:T(8,128)(2,1)} %tok.1, bf16[1536,384]{1,0:T(8,128)(2,1)} %wq.1, bf16[1536,384]{1,0:T(8,128)(2,1)} %wk.1, bf16[1536,384]{1,0:T(8,128)(2,1)} %wv.1, bf16[384,1536]{1,0:T(8,128)(2,1)} %wout.1, s32[4,6]{1,0:T(4,128)} %offs.1), custom_call_target="tpu_custom_call" | custom-call | tf_op jit(solution)/shard_map/pallas_call | solution.py:557
  59.7 1.6 %copy.8 = bf16[64,1536]{1,0:T(8,128)(2,1)} copy(bf16[64,1536]{1,0:T(8,128)(2,1)} %shard_map.64) | data formatting | bytes 393216

commit v6 on v5

--- a/solution.py
+++ b/solution.py
@@ -72,10 +72,9 @@
     own_w = pl.ds(pl.multiple_of(384 * hd, 128), 384)
     load_tok = pltpu.make_async_copy(tok, TOK, win.at[3])
     load_wout = pltpu.make_async_copy(wout, WF.at[own_w], win.at[4])
-    load_tok.start()
     for c in loads:
         c.start()
-    load_wout.start()
+    load_tok.start()
 
     def rcopy(src, dst, ssem, rsem, dev):
         return pltpu.make_async_remote_copy(
@@ -113,12 +112,11 @@
     def other_rows(sub):
         return pl.ds(pl.multiple_of(HALF - lo + sub * 64, 64), 64)
 
-    load_tok.wait()
     pl.semaphore_wait(barrier, 7)
     sends = []
 
     def own(sub, part, n):
-        c = rcopy(TOK.at[rows_of(sub, part)], T.at[0, rows_of(sub, part)], ts.at[n], tr.at[n], n_out)
+        c = rcopy(tok.at[rows_of(sub, part)], T.at[0, rows_of(sub, part)], ts.at[n], tr.at[n], n_out)
         c.start()
         sends.append(c)
 
@@ -131,6 +129,7 @@
 
     for c in loads:
         c.wait()
+    load_tok.wait()
 
     def mover(rows, with_part):
         r = lax.broadcasted_iota(jnp.int32, (rows, 384), 0)
@@ -151,6 +150,8 @@
         for h in range(3):
             W3[h, r, 0:128] = wkv[:, h * 128:(h + 1) * 128].astype(BF)
             W3[h, r, 128:256] = wqq[:, h * 128:(h + 1) * 128].astype(BF)
+
+    load_wout.start()
 
     def targets(h, i):
         o1 = offs[1, 3 * par + h] & 1

time: 61.5 us -> 61.7 us (level)
  no operation moved by 1% of the time
where the time goes in v6:
time: 61.7 us; the launch traced here: 61.6 us
  Pallas kernels  60 us (97%)
  local copies, waits for them, and re-layouts  1.62 us (3%)
    pallas_call x1, Pallas kernels, local(): pl.pallas_call(body, out_shape=jax.ShapeDtypeStruct((64, D), BF), in_spec...  60 us
    unnamed x1, local copies, waits for them, and re-layouts  1.62 us

profile of v6, /device:TPU:1, one launch (start us, length us, event | category | flops | bytes accessed | tf_op | source)
XLA Modules:
  0.0 61.6 jit_solution(7576554949156028657)
XLA Ops:
  0.0 60.0 %shard_map.64 = bf16[64,1536]{1,0:T(8,128)(2,1)} custom-call(bf16[256,1536]{1,0:T(8,128)(2,1)} %tok.1, bf16[1536,384]{1,0:T(8,128)(2,1)} %wq.1, bf16[1536,384]{1,0:T(8,128)(2,1)} %wk.1, bf16[1536,384]{1,0:T(8,128)(2,1)} %wv.1, bf16[384,1536]{1,0:T(8,128)(2,1)} %wout.1, s32[4,6]{1,0:T(4,128)} %offs.1), custom_call_target="tpu_custom_call" | custom-call | tf_op jit(solution)/shard_map/pallas_call | solution.py:558
  60.0 1.6 %copy.8 = bf16[64,1536]{1,0:T(8,128)(2,1)} copy(bf16[64,1536]{1,0:T(8,128)(2,1)} %shard_map.64) | data formatting | bytes 393216

commit v7 on v6

--- a/solution.py
+++ b/solution.py
@@ -382,7 +382,14 @@
     share(2, 1 - zl, 5)
     shared(2, zl, 4)
     shared(2, 1 - zl, 5)
-    project(T.at[2], (zh + 2) % 4)
+    far_blk = (zh + 2) % 4
+    xs_far = T[2]
+    for h in range(3):
+        z = mm(sel(h), mm(xs_far, W3[h, :, 0:128]).astype(BF)).astype(BF)
+        ZKV1[h, far_blk] = z[0:128]
+        ZKV2[h, far_blk] = z[128:192]
+        ZKV3[h, far_blk] = z[192:224]
+        send(*l1_kv(far_blk, h))
     far_levels((zh + 2) % 4)
 
     load_wout.wait()

time: 61.7 us -> 61.7 us (level)
  no operation moved by 1% of the time
where the time goes in v7:
time: 61.7 us; the launch traced here: 61.5 us
  Pallas kernels  59.9 us (97%)
  local copies, waits for them, and re-layouts  1.62 us (3%)
    pallas_call x1, Pallas kernels, local(): pl.pallas_call(body, out_shape=jax.ShapeDtypeStruct((64, D), BF), in_spec...  59.9 us
    unnamed x1, local copies, waits for them, and re-layouts  1.62 us

profile of v7, /device:TPU:1, one launch (start us, length us, event | category | flops | bytes accessed | tf_op | source)
XLA Modules:
  0.0 61.5 jit_solution(6922833771914133566)
XLA Ops:
  0.0 59.9 %shard_map.64 = bf16[64,1536]{1,0:T(8,128)(2,1)} custom-call(bf16[256,1536]{1,0:T(8,128)(2,1)} %tok.1, bf16[1536,384]{1,0:T(8,128)(2,1)} %wq.1, bf16[1536,384]{1,0:T(8,128)(2,1)} %wk.1, bf16[1536,384]{1,0:T(8,128)(2,1)} %wv.1, bf16[384,1536]{1,0:T(8,128)(2,1)} %wout.1, s32[4,6]{1,0:T(4,128)} %offs.1), custom_call_target="tpu_custom_call" | custom-call | tf_op jit(solution)/shard_map/pallas_call | solution.py:565
  59.9 1.6 %copy.8 = bf16[64,1536]{1,0:T(8,128)(2,1)} copy(bf16[64,1536]{1,0:T(8,128)(2,1)} %shard_map.64) | data formatting | bytes 393216
